TPU v7x, 512 devices: a whole 4x8x8 slice. The times are simulated.
512 devices in a mesh: expert: 64 (over y, x, core), dp: 8 (over z).
Axes of the slice: x: 4, y: 8, z: 8, core: 2. Of those that a mesh axis runs over, the one named last changes fastest.
Arguments:
- layer_input: bfloat16 [65536, 2048], P(('expert', 'dp')), may hold values from -6 to 6
- log_grad: bfloat16 [65536, 2048], P(('expert', 'dp')), may hold values from -6 to 6
- router_logits: float32 [65536, 64], P(('expert', 'dp')), may hold values from -6 to 250
- expert_ids: int32 [65536, 1], P(('expert', 'dp')), may hold values from 0 to 63, as said below
- router_weight: bfloat16 [64, 2048], replicated, may hold values from -0.125 to 0.125
- gate_weight: bfloat16 [64, 2048, 1408], P('expert', None, 'dp'), may hold values from -0.125 to 0.125
- up_weight: bfloat16 [64, 2048, 1408], P('expert', None, 'dp'), may hold values from -0.125 to 0.125
- down_weight: bfloat16 [64, 1408, 2048], P('expert', 'dp'), may hold values from -0.15625 to 0.15625
- saved_pre: bfloat16 [64, 64, 8, 3, 2, 1408], P('expert', None, None, None, None, 'dp'), may hold values from -6 to 6
- request_ids: int32 [512], P(('expert', 'dp')), may hold values from 0 to 127, as said below
- risk_points: int32 [512], P(('expert', 'dp')), may hold values from 0 to 8000
- cand_scores: float32 [512], P(('expert', 'dp')), may hold values from -402 to 250
Outputs:
- input_grad: bfloat16 [65536, 2048], P(('expert', 'dp'))
- router_grad: float32 [64, 2048], P(None, ('expert', 'dp'))
Inputs may be any that keep to these rules, and one draw needn't show every extreme that they name: `expert_ids`: in the rows of one candidate no expert appears more than 3 times, and one expert appears exactly 3 times in every candidate's rows. `request_ids`: every request id appears exactly 4 times.
All inputs are finite; a program needn't handle non-finite values.
Results may differ from a plain program's by a relative error of at most 0.014.
Values may be sent and summed in bfloat16 or wider, within the bound.
No kernel may reach another device: no remote copies, remote signals or barrier semaphores. Data moves between devices by JAX's collectives and lax.ppermute only.
A program may use at most 128 MiB of HBM per device.

v0:
```python
import jax
import jax.numpy as jnp
from jax import lax
from jax.sharding import PartitionSpec as P

BEAM = 4


NEG = -1e30


def joined(value, axis, join):
    pieces = jax.tree.map(lambda part: lax.all_gather(part, axis), value)
    head = jax.tree.map(lambda part: part[0], pieces)
    tail = jax.tree.map(lambda part: part[1:], pieces)
    subtotal, _ = lax.scan(lambda subtotal, slab: (join(subtotal, slab), None), head, tail)
    return subtotal


def combine_requests(left_part, right_part):
    peak_score = jnp.maximum(left_part[0], right_part[0])
    scale_left = jnp.exp(left_part[0] - peak_score)
    scale_right = jnp.exp(right_part[0] - peak_score)
    mass_sum = left_part[1] * scale_left + right_part[1] * scale_right
    loaded_sum = left_part[2] * scale_left + right_part[2] * scale_right
    return (peak_score, mass_sum, loaded_sum)


def local(
    layer_input,
    log_grad,
    router_logits,
    expert_ids,
    router_weight,
    gate_weight,
    up_weight,
    down_weight,
    saved_pre,
    request_ids,
    risk_points,
    cand_scores,
):
    dp_count = lax.axis_size("dp")
    requests = lax.axis_size("expert") * dp_count // BEAM
    experts = router_weight.shape[0]
    slot_count = saved_pre.shape[3]
    model_width = layer_input.shape[1]
    risk_value = risk_points[0].astype(jnp.float32) * 0.001
    cand_score = cand_scores[0]
    member = jnp.arange(requests, dtype=jnp.int32) == request_ids[0]
    own_terms = (
        jnp.where(member, cand_score, NEG),
        member.astype(jnp.float32),
        jnp.where(member, risk_value, 0.0),
    )
    peak_score, mass_sum, loaded_sum = joined(own_terms, ("expert", "dp"), combine_requests)
    own_peak = jnp.sum(jnp.where(member, peak_score, 0.0))
    own_mass = jnp.sum(jnp.where(member, mass_sum, 0.0))
    own_loaded = jnp.sum(jnp.where(member, loaded_sum, 0.0))
    cand_prob = jnp.exp(cand_score - own_peak) / own_mass
    cand_weight = cand_prob * (risk_value - own_loaded / own_mass)
    scaled = (cand_weight * log_grad.astype(jnp.float32)).astype(jnp.bfloat16)
    chosen = expert_ids[:, 0]
    one_hot = (chosen[:, None] == jnp.arange(experts, dtype=jnp.int32)[None, :]).astype(jnp.int32)
    slot_rank = jnp.sum(one_hot * (jnp.cumsum(one_hot, axis=0) - 1), axis=1)
    target = chosen * slot_count + slot_rank
    placer = (jnp.arange(experts * slot_count, dtype=jnp.int32)[:, None] == target[None, :]).astype(
        jnp.bfloat16
    )
    outgoing = jnp.dot(placer, scaled, preferred_element_type=jnp.float32).astype(jnp.bfloat16)
    outgoing = outgoing.reshape(experts, slot_count, model_width)
    expert_rows = lax.all_to_all(outgoing, "expert", split_axis=0, concat_axis=0, tiled=True)
    arrived = lax.all_gather(expert_rows[:, None], "dp", axis=1, tiled=True)
    slot_rows = arrived.reshape(-1, model_width)
    saved_rows = saved_pre.reshape(slot_rows.shape[0], 2, saved_pre.shape[-1])
    gate_pre = saved_rows[:, 0].astype(jnp.float32)
    up_pre = saved_rows[:, 1].astype(jnp.float32)
    down_grad = jnp.einsum(
        "rd,fd->rf", slot_rows, down_weight[0], preferred_element_type=jnp.float32
    )
    sigmoid_a = jax.nn.sigmoid(gate_pre)
    silu_a = gate_pre * sigmoid_a
    gate_parts = jnp.sum(down_grad * (silu_a * up_pre), axis=1).astype(jnp.bfloat16)
    grad_a = (down_grad * up_pre * sigmoid_a * (1.0 + gate_pre * (1.0 - sigmoid_a))).astype(
        jnp.bfloat16
    )
    grad_b = (down_grad * silu_a).astype(jnp.bfloat16)
    partial_value = jnp.einsum(
        "rf,df->rd", grad_a, gate_weight[0], preferred_element_type=jnp.float32
    )
    partial_value = partial_value + jnp.einsum(
        "rf,df->rd", grad_b, up_weight[0], preferred_element_type=jnp.float32
    )
    partial_value = partial_value.astype(jnp.bfloat16).reshape(arrived.shape)
    gate_parts = gate_parts.reshape(arrived.shape[:3])
    summed, gathered_parts = (
        lax.all_to_all(partial_value, "dp", split_axis=1, concat_axis=1, tiled=True),
        lax.all_to_all(gate_parts, "dp", split_axis=1, concat_axis=1, tiled=True),
    )
    routed = jnp.sum(summed.astype(jnp.float32), axis=1).astype(jnp.bfloat16)
    gate_sum = jnp.sum(gathered_parts.astype(jnp.float32), axis=1).astype(jnp.bfloat16)
    homeward, home_grad = (
        lax.all_to_all(routed, "expert", split_axis=0, concat_axis=0, tiled=True),
        lax.all_to_all(gate_sum, "expert", split_axis=0, concat_axis=0, tiled=True),
    )
    routed_tok = jnp.einsum(
        "st,sd->td", placer, homeward.reshape(-1, model_width), preferred_element_type=jnp.float32
    )
    grad_tok = jnp.einsum(
        "st,s->t", placer, home_grad.reshape(-1), preferred_element_type=jnp.float32
    )
    chosen_mark = one_hot.astype(jnp.float32)
    peak_logit = jnp.max(router_logits, axis=1, keepdims=True)
    expd = jnp.exp(router_logits - peak_logit)
    router_prob = expd / jnp.sum(expd, axis=1, keepdims=True)
    chosen_prob = jnp.sum(router_prob * chosen_mark, axis=1)
    logit_grad = ((grad_tok * chosen_prob)[:, None] * (chosen_mark - router_prob)).astype(
        jnp.bfloat16
    )
    input_grad = (
        chosen_prob[:, None] * routed_tok
        + jnp.dot(logit_grad, router_weight, preferred_element_type=jnp.float32)
    ).astype(jnp.bfloat16)
    router_part = jnp.einsum(
        "te,td->ed", logit_grad, layer_input, preferred_element_type=jnp.float32
    )
    router_grad = lax.psum_scatter(router_part, ("expert", "dp"), scatter_dimension=1, tiled=True)
    return (input_grad, router_grad)


def solution(mesh):
    return jax.shard_map(
        local,
        mesh=mesh,
        in_specs=(
            P(("expert", "dp"), None),
            P(("expert", "dp"), None),
            P(("expert", "dp"), None),
            P(("expert", "dp"), None),
            P(),
            P("expert", None, "dp"),
            P("expert", None, "dp"),
            P("expert", "dp", None),
            P("expert", None, None, None, None, "dp"),
            P(("expert", "dp")),
            P(("expert", "dp")),
            P(("expert", "dp")),
        ),
        out_specs=(P(("expert", "dp"), None), P(None, ("expert", "dp"))),
        check_vma=False,
    )
```

profile of v0, /device:TPU:1, one launch (start us, length us, event | category | flops | bytes accessed | tf_op | source)
XLA Modules:
  0.0 861.5 jit_solution(18150289300763378375)
XLA Ops:
  8.6 66.4 %all-gather.3 = f32[512,1,128]{2,1,0:T(1,128)S(1)} all-gather(f32[1,1,128]{2,1,0:T(1,128)S(1)} %select_bitcast_fusion), channel_id=1, replica_groups=mesh['expert'=64,'dp'=8] {'expert','dp'}, dimensions={0}, use_global_device_ids=true | all-gather | bytes 262656 | tf_op jit(solution)/shard_map/all_gather | solution.py:13
  75.7 60.7 %all-gather.1 = f32[512,1,128]{2,1,0:T(1,128)S(1)} all-gather(f32[1,1,128]{2,1,0:T(1,128)S(1)} %select_bitcast_fusion.1), channel_id=1, replica_groups=mesh['expert'=64,'dp'=8] {'expert','dp'}, dimensions={0}, use_global_device_ids=true | all-gather | bytes 262656 | tf_op jit(solution)/shard_map/all_gather | solution.py:13
  136.4 60.1 %all-gather.2 = f32[512,1,128]{2,1,0:T(1,128)S(1)} all-gather(f32[1,1,128]{2,1,0:T(1,128)S(1)} %convert_bitcast_fusion), channel_id=1, replica_groups=mesh['expert'=64,'dp'=8] {'expert','dp'}, dimensions={0}, use_global_device_ids=true | all-gather | bytes 262656 | tf_op jit(solution)/shard_map/all_gather | solution.py:13
  196.7 40.1 %while.14 = (s32[]{:T(128)}, f32[128]{0:T(128)S(1)}, f32[128]{0:T(128)S(1)}, f32[128]{0:T(128)S(1)}, f32[511,128]{1,0:T(8,128)S(1)}, /*index=5*/f32[511,128]{1,0:T(8,128)S(1)}, f32[511,128]{1,0:T(8,128)S(1)}, s32[]{:T(128)}) while((s32[]{:T(128)}, f32[128]{0:T(128)S(1)}, f32[128]{0:T(128)S(1)}, f32[128]{0:T(128)S(1)}, ...), condition=%wide.region_6.7_spmd, body=%wide.region_5.6_spmd.sunk | while | flops 1410 | bytes 7261 | solution.py:16
  236.8 0.6 select_reduce_fusion.1
  238.7 0.6 select_reduce_fusion.3
  240.7 0.1 fusion.29
  240.8 0.2 reduce_window_sum.11
  241.0 0.2 select_reduce_fusion
  241.2 0.4 convolution_convert_fusion
  241.5 0.5 reshape.65
  242.1 36.5 %all_to_all.29 = bf16[64,3,2048]{2,1,0:T(4,128)(2,1)S(1)} all-to-all(bf16[64,3,2048]{2,1,0:T(4,128)(2,1)S(1)} %reshape.65), channel_id=1, replica_groups=mesh['expert'=64,'dp'=8] {'expert'}, dimensions={0} | all-to-all | bytes 1572864 | tf_op jit(solution)/shard_map/all_to_all | solution.py:72
  278.5 1.5 copy.43
  280.0 3.5 fusion.39
  283.5 3.5 copy.55
  287.1 0.9 copy.54
  288.0 64.7 %all-gather.6.cloned.1.call-done = bf16[64,24,2048]{2,0,1:T(8,128)(2,1)} async-done(((bf16[64,3,2048]{2,0,1:T(8,128)(2,1)}), bf16[64,24,2048]{2,0,1:T(8,128)(2,1)}) %all-gather.6.cloned.1.call-update) | async-done | bytes 6291472 | tf_op jit(solution)/shard_map/all_gather | solution.py:73
  352.7 6.3 copy.44
  359.0 2.4 fusion.14
  361.4 0.3 convert_element_type.83
  361.7 0.8 copy.49
  362.4 3.9 all-to-all-start.3
  366.3 2.0 fusion.20
  368.3 4.6 add_convert_fusion
  372.9 16.8 %reshape.68 = bf16[64,8,3,2048]{3,2,1,0:T(4,128)(2,1)} reshape(bf16[1536,2048]{1,0:T(8,128)(2,1)} %add_convert_fusion) | data formatting | bytes 12582912 | tf_op jit(solution)/shard_map/reshape | solution.py:94
  389.7 10.8 %copy.47 = bf16[64,8,3,2048]{3,0,2,1:T(8,128)(2,1)} copy(bf16[64,8,3,2048]{3,2,1,0:T(4,128)(2,1)} %reshape.68) | data formatting | bytes 12582912 | tf_op jit(solution)/shard_map/reshape | solution.py:94
  400.5 6.6 all-to-all-start.1
  407.1 0.7 copy.50
  407.9 141.3 %all-to-all-done.1 = bf16[64,8,3,2048]{3,0,2,1:T(8,128)(2,1)} async-done(((bf16[64,8,3,2048]{3,0,2,1:T(8,128)(2,1)}), bf16[64,8,3,2048]{3,0,2,1:T(8,128)(2,1)}, u32[]{:S(2)}, u32[]{:S(2)}) %all-to-all-start.1) | async-done | bytes 6291488 | tf_op jit(solution)/shard_map/all_to_all | solution.py:97
  549.2 10.3 %all-to-all-start.4 = ((bf16[64,1,3]{2,1,0:T(2,128)(2,1)}), bf16[64,1,3]{2,1,0:T(2,128)(2,1)S(1)}, u32[]{:S(2)}, u32[]{:S(2)}) async-start(bf16[64,1,3]{2,1,0:T(2,128)(2,1)} %copy.50), calls=%async_computation.4 | async-start | bytes 65536 | tf_op jit(solution)/shard_map/all_to_all | solution.py:104
  559.5 4.0 reduce_sum.93
  563.6 1.7 copy.48
  565.3 3.6 all-to-all-done.4
  568.8 6.9 all-to-all-start.2
  575.7 0.0 all-reduce.3.cloned.1.call-start
  575.8 0.1 copy.42
  575.9 0.2 fusion.31
  576.1 0.2 multiply_reduce_fusion
  576.3 0.1 reduce.2
  576.4 0.2 reshape.90
  576.5 0.1 fusion.9
  576.7 1.4 fusion.37
  578.1 272.5 %all-reduce.3.cloned.1.call-done = f32[64,2048]{0,1:T(8,128)} async-done(((f32[64,2048]{0,1:T(8,128)}), f32[64,2048]{0,1:T(8,128)}) %all-reduce.3.cloned.1.call-update) | async-done | bytes 524304
  850.6 1.3 constant_dynamic-slice_fusion.3
  851.9 0.7 reshape.69
  852.6 0.4 convolution_multiply_fusion
  853.0 0.6 copy-done.7
  853.5 1.2 fusion.8
  (1574 shorter events, 28.0 us)
Async XLA Ops:
  7.2 359.1 %copy-start = (bf16[1,2048,176]{1,2,0:T(8,128)(2,1)S(1)}, bf16[1,2048,176]{1,2,0:T(8,128)(2,1)}, u32[]{:S(2)}) copy-start(bf16[1,2048,176]{1,2,0:T(8,128)(2,1)} %param.19) | copy-start | bytes 2162692
  7.2 345.5 %all-gather.6.cloned.1.call-start = ((), (), s32[]{:S(2)}) async-start(), calls=%async_computation.5 | async-start | bytes 7077888 | tf_op jit(solution)/shard_map/all_gather | solution.py:73
  196.6 44.1 %copy-start.9 = (s32[128,1]{0,1:T(1,128)S(1)}, s32[128,1]{0,1:T(1,128)}, u32[]{:S(2)}) copy-start(s32[128,1]{0,1:T(1,128)} %param.17) | copy-start | bytes 1540
  196.6 44.6 %copy-start.5 = (bf16[128,2048]{1,0:T(8,128)(2,1)S(1)}, bf16[128,2048]{1,0:T(8,128)(2,1)}, u32[]{:S(2)}) copy-start(bf16[128,2048]{1,0:T(8,128)(2,1)} %param.15) | copy-start | bytes 1572868
  278.5 1.5 copy-start.2
  283.5 3.5 copy-start.3
  352.7 6.3 copy-start.10
  362.4 38.1 %all-to-all-start.3 = ((bf16[64,8,3]{0,2,1:T(4,128)(2,1)}), bf16[64,8,3]{0,2,1:T(4,128)(2,1)S(1)}, u32[]{:S(2)}, u32[]{:S(2)}) async-start(bf16[64,8,3]{0,2,1:T(4,128)(2,1)} %copy.49), calls=%async_computation.3 | async-start | bytes 16384 | tf_op jit(solution)/shard_map/all_to_all | solution.py:98
  366.3 2.0 copy-start.4
  400.5 148.7 %all-to-all-start.1 = ((bf16[64,8,3,2048]{3,0,2,1:T(8,128)(2,1)}), bf16[64,8,3,2048]{3,0,2,1:T(8,128)(2,1)}, u32[]{:S(2)}, u32[]{:S(2)}) async-start(bf16[64,8,3,2048]{3,0,2,1:T(8,128)(2,1)} %copy.47), calls=%async_computation.1 | async-start | bytes 12582912 | tf_op jit(solution)/shard_map/all_to_all | solution.py:97
  549.2 19.6 %all-to-all-start.4 = ((bf16[64,1,3]{2,1,0:T(2,128)(2,1)}), bf16[64,1,3]{2,1,0:T(2,128)(2,1)S(1)}, u32[]{:S(2)}, u32[]{:S(2)}) async-start(bf16[64,1,3]{2,1,0:T(2,128)(2,1)} %copy.50), calls=%async_computation.4 | async-start | bytes 65536 | tf_op jit(solution)/shard_map/all_to_all | solution.py:104
  565.3 10.5 %copy-start.8 = (f32[128,64]{0,1:T(8,128)S(1)}, f32[128,64]{0,1:T(8,128)}, u32[]{:S(2)}) copy-start(f32[128,64]{0,1:T(8,128)} %param.16) | copy-start | bytes 98308
  565.3 11.4 %copy-start.6 = (bf16[128,2048]{1,0:T(8,128)(2,1)S(1)}, bf16[128,2048]{1,0:T(8,128)(2,1)}, u32[]{:S(2)}) copy-start(bf16[128,2048]{1,0:T(8,128)(2,1)} %param.14) | copy-start | bytes 1572868
  568.8 283.1 %all-to-all-start.2 = ((bf16[64,3,2048]{2,1,0:T(4,128)(2,1)}), bf16[64,3,2048]{2,1,0:T(4,128)(2,1)S(1)}, u32[]{:S(2)}, u32[]{:S(2)}) async-start(bf16[64,3,2048]{2,1,0:T(4,128)(2,1)} %copy.48), calls=%async_computation.2 | async-start | bytes 2097152 | tf_op jit(solution)/shard_map/all_to_all | solution.py:103
  575.7 274.9 %all-reduce.3.cloned.1.call-start = ((), (), s32[]{:S(2)}) async-start(), calls=%async_computation.6 | async-start | bytes 2097152
  852.6 1.0 copy-start.7
  852.6 2.1 copy-start.1
Sparse Core Ops, SparseCore 0:
  280.1 72.5 all-gather.5
  581.6 268.9 all-reduce.2
where the time goes:
time: 863 us; the launch traced here: 862 us
  waiting for transfers between devices  482 us (56%)
  blocking collectives  224 us (26%)
  local copies, waits for them, and re-layouts  51.5 us (6%)
  other arithmetic  32.6 us (4%)
  starting transfers between devices  27.7 us (3%)
  between operations  19.1 us (2%)
  loops' own time  12.4 us (1%)
  matrix products  12.4 us (1%)
    unnamed x3, waiting for transfers between devices  273 us
    all_gather x3, blocking collectives, joined(): pieces = jax.tree.map(lambda part: lax.all_gather(part, axis), value)  187 us
    all_to_all x1, waiting for transfers between devices, local(): lax.all_to_all(partial_value, 'dp', split_axis=1, concat_axis=1, tiled=True)  141 us
    all_gather x1, waiting for transfers between devices, local(): arrived = lax.all_gather(expert_rows[:, None], 'dp', axis=1, tiled=True)  64.7 us
    all_to_all x1, blocking collectives, local(): lax.all_to_all(outgoing, 'expert', split_axis=0, concat_axis=0, tiled=True)  36.5 us
    reshape x2, local copies, waits for them, and re-layouts, local(): partial_value = partial_value.astype(jnp.bfloat16).reshape(arrived.shape)  27.6 us
  transfers between devices with their start and end apart: 6, of which 4 were waited for; matrix products, arithmetic and copies ran while one was open for 6% of the time, Pallas kernels for 0%

commit v1 on v0

v1 whole, which is shorter than its diff:
```python
import jax
import jax.numpy as jnp
from jax import lax
from jax.sharding import PartitionSpec as P

NEG = -1e30


def local(
    layer_input,
    log_grad,
    router_logits,
    expert_ids,
    router_weight,
    gate_weight,
    up_weight,
    down_weight,
    saved_pre,
    request_ids,
    risk_points,
    cand_scores,
):
    expert_count = lax.axis_size("expert")
    dp_count = lax.axis_size("dp")
    experts = router_weight.shape[0]
    cap = saved_pre.shape[3]
    hidden = saved_pre.shape[5]
    width = layer_input.shape[1]
    rows = expert_count * cap
    f32, bf16 = jnp.float32, jnp.bfloat16

    down_full = lax.all_gather(down_weight[0], "dp", axis=0, tiled=True)

    chosen = expert_ids[:, 0]
    one_hot = (chosen[:, None] == jnp.arange(experts, dtype=jnp.int32)[None, :]).astype(jnp.int32)
    slot_rank = jnp.sum(one_hot * (jnp.cumsum(one_hot, axis=0) - 1), axis=1)
    target = chosen * cap + slot_rank
    placer = (jnp.arange(experts * cap, dtype=jnp.int32)[:, None] == target[None, :]).astype(bf16)
    outgoing = jnp.dot(placer, log_grad, preferred_element_type=f32).astype(bf16)
    expert_rows = lax.all_to_all(
        outgoing.reshape(experts, cap, width), "expert", split_axis=0, concat_axis=0, tiled=True
    )

    risk_value = risk_points[0].astype(f32) * 0.001
    lane = jnp.arange(128, dtype=jnp.int32)
    record = jnp.where(
        lane == 0,
        request_ids[0].astype(f32),
        jnp.where(lane == 1, cand_scores[0], jnp.where(lane == 2, risk_value, 0.0)),
    )
    records = jnp.broadcast_to(record[None, None, :], (expert_count, 1, 128))
    records = lax.all_to_all(records, "expert", split_axis=0, concat_axis=0, tiled=True)
    records = jnp.broadcast_to(records.reshape(1, expert_count, 128), (dp_count, expert_count, 128))
    records = lax.all_to_all(records, "dp", split_axis=0, concat_axis=0, tiled=True)
    expert_rows, records, down_full, saved_pre = lax.optimization_barrier(
        (expert_rows, records, down_full, saved_pre)
    )
    member = records[:, :, 0:1] == request_ids[0].astype(f32)
    scores = records[:, :, 1:2]
    peak = jnp.max(jnp.where(member, scores, NEG))
    lifted = jnp.where(member, jnp.exp(jnp.where(member, scores, NEG) - peak), 0.0)
    mass = jnp.sum(lifted)
    loaded = jnp.sum(lifted * records[:, :, 2:3])
    cand_weight = jnp.exp(cand_scores[0] - peak) / mass * (risk_value - loaded / mass)

    slot_rows = expert_rows.reshape(rows, width)
    down_grad = jnp.einsum("fd,rd->fr", down_full, slot_rows, preferred_element_type=f32)
    down_grad = down_grad.astype(bf16).reshape(dp_count, hidden, rows)
    down_grad = lax.all_to_all(down_grad, "dp", split_axis=0, concat_axis=0, tiled=True)
    down_grad = down_grad.astype(f32)

    saved = jnp.transpose(saved_pre[0], (3, 1, 4, 0, 2)).reshape(2, dp_count, hidden, rows)
    gate_pre = saved[0].astype(f32)
    up_pre = saved[1].astype(f32)
    sigmoid_a = jax.nn.sigmoid(gate_pre)
    silu_a = gate_pre * sigmoid_a
    gate_parts = jnp.sum(down_grad * (silu_a * up_pre), axis=1)
    grad_a = (down_grad * up_pre * sigmoid_a * (1.0 + gate_pre * (1.0 - sigmoid_a))).astype(bf16)
    grad_b = (down_grad * silu_a).astype(bf16)
    part = jnp.einsum("zfr,df->zrd", grad_a, gate_weight[0], preferred_element_type=f32)
    part = part + jnp.einsum("zfr,df->zrd", grad_b, up_weight[0], preferred_element_type=f32)
    part = part.astype(bf16).reshape(dp_count * rows, width)
    routed = lax.psum_scatter(part, "dp", scatter_dimension=0, tiled=True)

    gate_sum = lax.all_to_all(gate_parts, "dp", split_axis=0, concat_axis=0, tiled=True)
    gate_sum = jnp.sum(gate_sum, axis=0).reshape(expert_count, 1, cap)
    home_grad = lax.all_to_all(gate_sum, "expert", split_axis=0, concat_axis=0, tiled=True)
    home_grad = home_grad.reshape(rows).astype(bf16)
    grad_tok = jnp.einsum("st,s->t", placer, home_grad, preferred_element_type=f32)

    chosen_mark = one_hot.astype(f32)
    peak_logit = jnp.max(router_logits, axis=1, keepdims=True)
    expd = jnp.exp(router_logits - peak_logit)
    router_prob = expd / jnp.sum(expd, axis=1, keepdims=True)
    chosen_prob = jnp.sum(router_prob * chosen_mark, axis=1) * cand_weight
    logit_grad = ((grad_tok * chosen_prob)[:, None] * (chosen_mark - router_prob)).astype(bf16)

    router_part = jnp.einsum("td,te->de", layer_input, logit_grad, preferred_element_type=f32)
    share = width // expert_count
    router_part = router_part.reshape(expert_count, share, experts)
    router_part = lax.all_to_all(router_part, "expert", split_axis=0, concat_axis=0, tiled=True)
    router_part = jnp.sum(router_part, axis=0).reshape(dp_count, share // dp_count, experts)
    router_part = lax.all_to_all(router_part, "dp", split_axis=0, concat_axis=0, tiled=True)
    router_grad = jnp.sum(router_part, axis=0).T

    homeward = lax.all_to_all(
        routed.reshape(expert_count, cap, width), "expert", split_axis=0, concat_axis=0, tiled=True
    )
    routed_tok = jnp.einsum(
        "st,sd->td", placer, homeward.reshape(rows, width), preferred_element_type=f32
    )
    input_grad = (
        chosen_prob[:, None] * routed_tok
        + jnp.dot(logit_grad, router_weight, preferred_element_type=f32)
    ).astype(bf16)
    return (input_grad, router_grad)


def solution(mesh):
    return jax.shard_map(
        local,
        mesh=mesh,
        in_specs=(
            P(("expert", "dp"), None),
            P(("expert", "dp"), None),
            P(("expert", "dp"), None),
            P(("expert", "dp"), None),
            P(),
            P("expert", None, "dp"),
            P("expert", None, "dp"),
            P("expert", "dp", None),
            P("expert", None, None, None, None, "dp"),
            P(("expert", "dp")),
            P(("expert", "dp")),
            P(("expert", "dp")),
        ),
        out_specs=(P(("expert", "dp"), None), P(None, ("expert", "dp"))),
        check_vma=False,
    )
```

time: 863 us -> 265 us (0.31)
  waiting for transfers between devices: 482 us -> 85.6 us
  blocking collectives: 224 us -> 54.9 us
  local copies, waits for them, and re-layouts: 51.5 us -> 18.5 us
  starting transfers between devices: 27.7 us -> 56.7 us
  other arithmetic: 32.6 us -> 14.9 us
  loops' own time: 12.4 us -> 0 us
    unnamed x3 -> x2, waiting for transfers between devices: 273 us -> 0.7 us
    all_gather x3 -> x0, blocking collectives: 187 us -> none  [joined(): pieces = jax.tree.map(lambda part: lax.all_gather(part, axis), value)]
    all_to_all x3 -> x6, waiting for transfers between devices: 141 us -> 66.1 us  [the longest x1 26.6 us: local(): lax.all_to_all(routed.reshape(expert_count, cap, width), 'expert', split_...]
    all_gather x1, waiting for transfers between devices: 64.7 us -> 4.48 us  [local(): down_full = lax.all_gather(down_weight[0], 'dp', axis=0, tiled=True)]
    add x1023 -> x1, other arithmetic: 26.4 us -> 0.01 us  [local(): target = chosen * cap + slot_rank]
    all_to_all x3 -> x6, starting transfers between devices: 17.4 us -> 43.2 us  [the longest x1 11.6 us: local(): lax.all_to_all(records, 'expert', split_axis=0, concat_axis=0, tiled=True)]
    reshape x5 -> x6, local copies, waits for them, and re-layouts: 28.9 us -> 6.41 us  [the longest x1 3.28 us: local(): routed.reshape(expert_count, cap, width)]
    all_to_all x1 -> x2, blocking collectives: 36.5 us -> 54.9 us  [the longest x1 33 us: local(): lax.all_to_all(outgoing.reshape(experts, cap, width), 'expert', split_axi...]
  transfers between devices with their start and end apart: 6 -> 9, of which waited for: 4 -> 8; matrix products, arithmetic and copies ran while one was open for 6% -> 10% of each run, Pallas kernels for 0% -> 0%
where the time goes in v1:
time: 265 us; the launch traced here: 264 us
  waiting for transfers between devices  85.6 us (32%)
  starting transfers between devices  56.7 us (21%)
  blocking collectives  54.9 us (21%)
  between operations  18.9 us (7%)
  local copies, waits for them, and re-layouts  18.5 us (7%)
  other arithmetic  14.9 us (6%)
  matrix products  14.4 us (5%)
    all_to_all x1, blocking collectives, local(): lax.all_to_all(outgoing.reshape(experts, cap, width), 'expert', split_axi...  33 us
    all_to_all x1, waiting for transfers between devices, local(): lax.all_to_all(routed.reshape(expert_count, cap, width), 'expert', split_...  26.6 us
    all_to_all x1, blocking collectives, local(): lax.all_to_all(router_part, 'expert', split_axis=0, concat_axis=0, tiled=...  22 us
    all_to_all x1, waiting for transfers between devices, local(): lax.all_to_all(down_grad, 'dp', split_axis=0, concat_axis=0, tiled=True)  16.3 us
    all_to_all x1, waiting for transfers between devices, local(): lax.all_to_all(records, 'dp', split_axis=0, concat_axis=0, tiled=True)  13.7 us
    all_to_all x1, starting transfers between devices, local(): lax.all_to_all(gate_sum, 'expert', split_axis=0, concat_axis=0, tiled=True)  13.2 us
    all_to_all x1, starting transfers between devices, local(): lax.all_to_all(records, 'expert', split_axis=0, concat_axis=0, tiled=True)  11.6 us
    all_to_all x1, starting transfers between devices, local(): lax.all_to_all(routed.reshape(expert_count, cap, width), 'expert', split_...  10.5 us
  transfers between devices with their start and end apart: 9, of which 8 were waited for; matrix products, arithmetic and copies ran while one was open for 10% of the time, Pallas kernels for 0%

profile of v1, /device:TPU:1, one launch (start us, length us, event | category | flops | bytes accessed | tf_op | source)
XLA Modules:
  0.0 263.9 jit_solution(3016934606211808545)
XLA Ops:
  7.2 0.7 all-gather.3.cloned.1.call-update
  9.9 0.6 broadcast_in_dim.47
  10.5 11.6 %all-to-all-start.1 = ((f32[64,1,128]{2,1,0:T(1,128)}), f32[64,1,128]{2,1,0:T(1,128)S(1)}, u32[]{:S(2)}, u32[]{:S(2)}) async-start(f32[64,1,128]{2,1,0:T(1,128)} %broadcast_in_dim.47), calls=%async_computation.1 | async-start | bytes 65536 | tf_op jit(solution)/shard_map/all_to_all | solution.py:52
  22.1 0.7 fusion.16
  23.1 0.8 select_reduce_fusion
  23.9 7.6 %all-to-all-done.1 = f32[64,1,128]{2,1,0:T(1,128)S(1)} async-done(((f32[64,1,128]{2,1,0:T(1,128)}), f32[64,1,128]{2,1,0:T(1,128)S(1)}, u32[]{:S(2)}, u32[]{:S(2)}) %all-to-all-start.1) | async-done | bytes 32800 | tf_op jit(solution)/shard_map/all_to_all | solution.py:52
  31.5 0.7 broadcast_in_dim.49
  32.2 10.0 %all-to-all-start.2 = ((f32[8,64,128]{2,1,0:T(8,128)}), f32[8,64,128]{2,1,0:T(8,128)S(1)}, u32[]{:S(2)}, u32[]{:S(2)}) async-start(f32[8,64,128]{2,1,0:T(8,128)} %broadcast_in_dim.49), calls=%async_computation.2 | async-start | bytes 524288 | tf_op jit(solution)/shard_map/all_to_all | solution.py:54
  43.1 13.7 %all-to-all-done.2 = f32[8,64,128]{2,1,0:T(8,128)S(1)} async-done(((f32[8,64,128]{2,1,0:T(8,128)}), f32[8,64,128]{2,1,0:T(8,128)S(1)}, u32[]{:S(2)}, u32[]{:S(2)}) %all-to-all-start.2) | async-done | bytes 262176 | tf_op jit(solution)/shard_map/all_to_all | solution.py:54
  56.8 33.0 %all_to_all.49 = bf16[64,3,2048]{2,1,0:T(4,128)(2,1)S(1)} all-to-all(bf16[64,3,2048]{2,1,0:T(4,128)(2,1)S(1)} %reshape.77), channel_id=1, replica_groups=mesh['expert'=64,'dp'=8] {'expert'}, dimensions={0} | all-to-all | bytes 1572864 | tf_op jit(solution)/shard_map/all_to_all | solution.py:40
  89.8 4.5 %all-gather.3.cloned.1.call-done = bf16[1,1408,2048]{2,1,0:T(8,128)(2,1)} async-done(((bf16[1,176,2048]{2,1,0:T(8,128)(2,1)}), bf16[1,1408,2048]{2,1,0:T(8,128)(2,1)}) %all-gather.3.cloned.1.call-update) | async-done | bytes 5767184 | tf_op jit(solution)/shard_map/all_gather | solution.py:32
  94.3 0.7 reshape.78
  94.9 4.7 %convolution_convert_fusion = bf16[1408,192]{0,1:T(8,128)(2,1)S(1)} fusion(bf16[1408,2048]{1,0:T(8,128)(2,1)} %bitcast.78, bf16[192,2048]{1,0:T(8,128)(2,1)S(1)} %reshape.78), kind=kOutput, calls=%fused_computation.1 | convolution fusion | flops 1107566592 | bytes 7094272 | tf_op jit(solution)/shard_map/fd,rd->fr/dot_general | solution.py:67
  99.6 1.1 copy.86
  100.8 4.2 %all-to-all-start.3 = ((bf16[8,176,192]{2,1,0:T(8,128)(2,1)}), bf16[8,176,192]{2,1,0:T(8,128)(2,1)}, u32[]{:S(2)}, u32[]{:S(2)}) async-start(bf16[8,176,192]{2,1,0:T(8,128)(2,1)} %bitcast.6), calls=%async_computation.3 | async-start | bytes 1441792 | tf_op jit(solution)/shard_map/all_to_all | solution.py:69
  105.2 0.5 copy.93
  106.1 0.9 copy.78
  107.1 2.1 copy.79
  109.1 16.3 %all-to-all-done.3 = bf16[8,176,192]{2,1,0:T(8,128)(2,1)} async-done(((bf16[8,176,192]{2,1,0:T(8,128)(2,1)}), bf16[8,176,192]{2,1,0:T(8,128)(2,1)}, u32[]{:S(2)}, u32[]{:S(2)}) %all-to-all-start.3) | async-done | bytes 540704 | tf_op jit(solution)/shard_map/all_to_all | solution.py:69
  125.4 1.8 copy.76
  127.2 3.4 %fusion.4 = (bf16[8,176,192]{1,0,2:T(8,128)(2,1)S(1)}, bf16[8,176,192]{1,0,2:T(8,128)(2,1)S(1)}, f32[8,176,192]{1,0,2:T(8,128)}) fusion(bf16[8,176,192]{1,0,2:T(8,128)(2,1)S(1)} %copy.76, f32[1,8,176,64,3]{2,1,4,3,0:T(8,128)} %copy.79, f32[1,8,176,64,3]{2,1,4,3,0:T(8,128)S(1)} %copy.78), kind=kLoop, calls=%fused_computation.13 | loop fusion | flops 3784704 | bytes 4866048 | tf_op jit(solution)/shard_map/convert_element_type | solution.py:79
  130.6 1.8 fusion.12
  132.4 4.5 %add_convert_fusion = bf16[8,192,2048]{2,1,0:T(8,128)(2,1)} fusion(f32[8,192,2048]{2,1,0:T(8,128)S(1)} %fusion.12, bf16[8,176,192]{1,0,2:T(8,128)(2,1)S(1)} %get-tuple-element.14, bf16[1,2048,176]{1,2,0:T(8,128)(2,1)S(1)} %copy-done.2), kind=kOutput, calls=%fused_computation | convolution fusion | flops 1113587712 | bytes 20135936 | tf_op jit(solution)/shard_map/zfr,df->zrd/dot_general | solution.py:81
  137.0 0.7 copy-done.5
  138.2 1.0 copy.72
  139.2 1.3 fusion.23
  140.6 1.7 fusion.5
  142.3 0.7 copy.82
  142.9 3.3 %all-to-all-start.5 = ((f32[8,1,192]{2,1,0:T(1,128)}), f32[8,1,192]{2,1,0:T(1,128)S(1)}, u32[]{:S(2)}, u32[]{:S(2)}) async-start(f32[8,1,192]{2,1,0:T(1,128)} %copy.82), calls=%async_computation.6 | async-start | bytes 16384 | tf_op jit(solution)/shard_map/all_to_all | solution.py:85
  146.2 2.0 fusion.22
  150.8 2.0 all-to-all-done.5
  152.9 0.6 convert.2
  153.5 13.2 %all-to-all-start.6 = ((bf16[64,1,3]{2,1,0:T(2,128)(2,1)}), bf16[64,1,3]{2,1,0:T(2,128)(2,1)S(1)}, u32[]{:S(2)}, u32[]{:S(2)}) async-start(bf16[64,1,3]{2,1,0:T(2,128)(2,1)} %convert.2), calls=%async_computation.7 | async-start | bytes 65536 | tf_op jit(solution)/shard_map/all_to_all | solution.py:87
  166.8 9.3 %all-to-all-done.6 = bf16[64,1,3]{2,1,0:T(2,128)(2,1)S(1)} async-done(((bf16[64,1,3]{2,1,0:T(2,128)(2,1)}), bf16[64,1,3]{2,1,0:T(2,128)(2,1)S(1)}, u32[]{:S(2)}, u32[]{:S(2)}) %all-to-all-start.6) | async-done | bytes 416 | tf_op jit(solution)/shard_map/all_to_all | solution.py:87
  176.4 1.4 convolution_bitcast_fusion
  178.2 0.7 reshape.95
  178.9 22.0 %all_to_all.50 = f32[64,1,2048]{2,1,0:T(1,128)S(1)} all-to-all(f32[64,1,2048]{2,1,0:T(1,128)S(1)} %reshape.95), channel_id=1, replica_groups=mesh['expert'=64,'dp'=8] {'expert'}, dimensions={0} | all-to-all | bytes 1048576 | tf_op jit(solution)/shard_map/all_to_all | solution.py:101
  201.4 1.9 reduce.3
  203.8 0.7 reshape.97
  204.5 3.6 %all-to-all-start.8 = ((f32[8,1,256]{2,1,0:T(1,128)}), f32[8,1,256]{2,1,0:T(1,128)S(1)}, u32[]{:S(2)}, u32[]{:S(2)}) async-start(f32[8,1,256]{2,1,0:T(1,128)} %reshape.97), calls=%async_computation.9 | async-start | bytes 16384 | tf_op jit(solution)/shard_map/all_to_all | solution.py:103
  208.1 5.0 %reduce-scatter.2.cloned.1.call-done = bf16[192,2048]{1,0:T(8,128)(2,1)} async-done(((bf16[1536,2048]{1,0:T(8,128)(2,1)}), bf16[192,2048]{1,0:T(8,128)(2,1)}) %reduce-scatter.2.cloned.1.call-update) | async-done | bytes 786448 | tf_op jit(solution)/shard_map/reduce_scatter | solution.py:83
  213.1 3.3 %reshape.81 = bf16[64,3,2048]{2,1,0:T(4,128)(2,1)} reshape(bf16[192,2048]{1,0:T(8,128)(2,1)} %reduce-scatter.2.cloned.1.call-done) | data formatting | bytes 1572864 | tf_op jit(solution)/shard_map/reshape | solution.py:107
  216.4 10.5 %all-to-all-start.4 = ((bf16[64,3,2048]{2,1,0:T(4,128)(2,1)}), bf16[64,3,2048]{2,1,0:T(4,128)(2,1)S(1)}, u32[]{:S(2)}, u32[]{:S(2)}) async-start(bf16[64,3,2048]{2,1,0:T(4,128)(2,1)} %reshape.81), calls=%async_computation.5 | async-start | bytes 2097152 | tf_op jit(solution)/shard_map/all_to_all | solution.py:106
  226.9 0.7 reduce.4
  227.7 0.6 reduce_sum.89
  228.3 26.6 %all-to-all-done.4 = bf16[64,3,2048]{2,1,0:T(4,128)(2,1)S(1)} async-done(((bf16[64,3,2048]{2,1,0:T(4,128)(2,1)}), bf16[64,3,2048]{2,1,0:T(4,128)(2,1)S(1)}, u32[]{:S(2)}, u32[]{:S(2)}) %all-to-all-start.4) | async-done | bytes 786464 | tf_op jit(solution)/shard_map/all_to_all | solution.py:106
  254.9 0.7 reshape.82
  255.9 1.2 fusion
  (39 shorter events, 4.6 us)
Async XLA Ops:
  7.2 123.5 %copy-start = (bf16[1,2048,176]{1,2,0:T(8,128)(2,1)S(1)}, bf16[1,2048,176]{1,2,0:T(8,128)(2,1)}, u32[]{:S(2)}) copy-start(bf16[1,2048,176]{1,2,0:T(8,128)(2,1)} %param.17) | copy-start | bytes 2162692
  7.2 35.0 %copy-start.6 = (s32[128,1]{0,1:T(1,128)S(1)}, s32[128,1]{0,1:T(1,128)}, u32[]{:S(2)}) copy-start(s32[128,1]{0,1:T(1,128)} %param.15) | copy-start | bytes 1540
  7.2 35.0 %copy-start.3 = (bf16[128,2048]{1,0:T(8,128)(2,1)S(1)}, bf16[128,2048]{1,0:T(8,128)(2,1)}, u32[]{:S(2)}) copy-start(bf16[128,2048]{1,0:T(8,128)(2,1)} %param.13) | copy-start | bytes 1572868
  7.2 87.1 %all-gather.3.cloned.1.call-start = ((), (), s32[]{:S(2)}) async-start(), calls=%async_computation.11 | async-start | bytes 6488064 | tf_op jit(solution)/shard_map/all_gather | solution.py:32
  10.5 20.9 %all-to-all-start.1 = ((f32[64,1,128]{2,1,0:T(1,128)}), f32[64,1,128]{2,1,0:T(1,128)S(1)}, u32[]{:S(2)}, u32[]{:S(2)}) async-start(f32[64,1,128]{2,1,0:T(1,128)} %broadcast_in_dim.47), calls=%async_computation.1 | async-start | bytes 65536 | tf_op jit(solution)/shard_map/all_to_all | solution.py:52
  32.2 24.6 %all-to-all-start.2 = ((f32[8,64,128]{2,1,0:T(8,128)}), f32[8,64,128]{2,1,0:T(8,128)S(1)}, u32[]{:S(2)}, u32[]{:S(2)}) async-start(f32[8,64,128]{2,1,0:T(8,128)} %broadcast_in_dim.49), calls=%async_computation.2 | async-start | bytes 524288 | tf_op jit(solution)/shard_map/all_to_all | solution.py:54
  99.6 5.6 %copy-start.1 = (bf16[1,64,8,3,2,176]{5,4,3,2,1,0:T(2,128)(2,1)S(1)}, bf16[1,64,8,3,2,176]{5,4,3,2,1,0:T(2,128)(2,1)}, u32[]{:S(2)}) copy-start(bf16[1,64,8,3,2,176]{5,4,3,2,1,0:T(2,128)(2,1)} %param.20) | copy-start | bytes 3244036
  100.8 24.7 %all-to-all-start.3 = ((bf16[8,176,192]{2,1,0:T(8,128)(2,1)}), bf16[8,176,192]{2,1,0:T(8,128)(2,1)}, u32[]{:S(2)}, u32[]{:S(2)}) async-start(bf16[8,176,192]{2,1,0:T(8,128)(2,1)} %bitcast.6), calls=%async_computation.3 | async-start | bytes 1441792 | tf_op jit(solution)/shard_map/all_to_all | solution.py:69
  105.0 108.1 %reduce-scatter.2.cloned.1.call-start = ((), (), s32[]{:S(2)}) async-start(), calls=%async_computation.10 | async-start | bytes 7077888 | tf_op jit(solution)/shard_map/reduce_scatter | solution.py:83
  130.6 1.8 copy-start.2
  137.0 0.8 copy-start.5
  142.9 9.8 %all-to-all-start.5 = ((f32[8,1,192]{2,1,0:T(1,128)}), f32[8,1,192]{2,1,0:T(1,128)S(1)}, u32[]{:S(2)}, u32[]{:S(2)}) async-start(f32[8,1,192]{2,1,0:T(1,128)} %copy.82), calls=%async_computation.6 | async-start | bytes 16384 | tf_op jit(solution)/shard_map/all_to_all | solution.py:85
  153.5 22.5 %all-to-all-start.6 = ((bf16[64,1,3]{2,1,0:T(2,128)(2,1)}), bf16[64,1,3]{2,1,0:T(2,128)(2,1)S(1)}, u32[]{:S(2)}, u32[]{:S(2)}) async-start(bf16[64,1,3]{2,1,0:T(2,128)(2,1)} %convert.2), calls=%async_computation.7 | async-start | bytes 65536 | tf_op jit(solution)/shard_map/all_to_all | solution.py:87
  204.5 11.9 %all-to-all-start.8 = ((f32[8,1,256]{2,1,0:T(1,128)}), f32[8,1,256]{2,1,0:T(1,128)S(1)}, u32[]{:S(2)}, u32[]{:S(2)}) async-start(f32[8,1,256]{2,1,0:T(1,128)} %reshape.97), calls=%async_computation.9 | async-start | bytes 16384 | tf_op jit(solution)/shard_map/all_to_all | solution.py:103
  216.4 38.5 %all-to-all-start.4 = ((bf16[64,3,2048]{2,1,0:T(4,128)(2,1)}), bf16[64,3,2048]{2,1,0:T(4,128)(2,1)S(1)}, u32[]{:S(2)}, u32[]{:S(2)}) async-start(bf16[64,3,2048]{2,1,0:T(4,128)(2,1)} %reshape.81), calls=%async_computation.5 | async-start | bytes 2097152 | tf_op jit(solution)/shard_map/all_to_all | solution.py:106
  228.3 27.7 %copy-start.4 = (bf16[64,2048]{1,0:T(8,128)(2,1)S(1)}, bf16[64,2048]{1,0:T(8,128)(2,1)}, u32[]{:S(2)}) copy-start(bf16[64,2048]{1,0:T(8,128)(2,1)} %param.16) | copy-start | bytes 786436
Sparse Core Ops, SparseCore 0:
  10.1 84.0 all-gather.2
  137.1 75.9 reduce-scatter.1

commit v2 on v1

v2 whole, which is shorter than its diff:
```python
import jax
import jax.numpy as jnp
from jax import lax
from jax.experimental import pallas as pl
from jax.experimental.pallas import tpu as pltpu
from jax.sharding import PartitionSpec as P

NEG = -1e30
LANES = 128
RECORD_ROWS = 8


def nt_dot(left, right):
    return lax.dot_general(left, right, (((1,), (1,)), ((), ())), preferred_element_type=jnp.float32)


def tn_dot(left, right):
    return lax.dot_general(left, right, (((0,), (0,)), ((), ())), preferred_element_type=jnp.float32)


def down_kernel(down_ref, rows_ref, record_ref, out_ref):
    hidden = down_ref.shape[0]
    half = hidden // 2
    rows = rows_ref.shape[0]
    bf16 = jnp.bfloat16
    full = nt_dot(down_ref[...], rows_ref[...])
    head = full[:, :LANES]
    tail = full[:, LANES:]
    tail = jnp.concatenate([tail[:half], tail[half:]], axis=1)
    pick = (
        lax.broadcasted_iota(jnp.int32, (RECORD_ROWS, LANES), 0)
        == lax.broadcasted_iota(jnp.int32, (RECORD_ROWS, LANES), 1)
    ).astype(bf16)
    record = nt_dot(pick, record_ref[...])
    record = jnp.concatenate([record, jnp.zeros_like(record)], axis=1)
    out_ref[0, :hidden, :] = head.astype(bf16)
    out_ref[0, hidden:, :] = jnp.concatenate([tail, record], axis=0).astype(bf16)


def up_kernel(packed_ref, scale_a_ref, scale_b_ref, scale_g_ref, gate_ref, up_ref, part_ref, gate_part_ref):
    hidden = gate_ref.shape[0]
    half = hidden // 2
    bf16 = jnp.bfloat16
    head = packed_ref[0, :hidden, :].astype(jnp.float32)
    tail = packed_ref[0, hidden:, :].astype(jnp.float32)[:half]
    side = LANES // 2
    tail = jnp.concatenate([tail[:, :side], tail[:, side:]], axis=0)
    down_grad = jnp.concatenate([head, tail], axis=1)
    gate_part_ref[0] = jnp.sum(down_grad * scale_g_ref[0], axis=0, keepdims=True)
    grad_a = (down_grad * scale_a_ref[0]).astype(bf16)
    grad_b = (down_grad * scale_b_ref[0]).astype(bf16)
    part_ref[0] = (tn_dot(grad_a, gate_ref[...]) + tn_dot(grad_b, up_ref[...])).astype(bf16)


def local(
    layer_input,
    log_grad,
    router_logits,
    expert_ids,
    router_weight,
    gate_weight,
    up_weight,
    down_weight,
    saved_pre,
    request_ids,
    risk_points,
    cand_scores,
):
    expert_count = lax.axis_size("expert")
    dp_count = lax.axis_size("dp")
    experts = router_weight.shape[0]
    cap = saved_pre.shape[3]
    hidden = saved_pre.shape[5]
    width = layer_input.shape[1]
    rows = expert_count * cap
    packed_rows = hidden + hidden // 2 + RECORD_ROWS
    f32, bf16 = jnp.float32, jnp.bfloat16

    down_full = lax.all_gather(down_weight[0], "dp", axis=0, tiled=True)

    score = cand_scores[0]
    score_hi = lax.reduce_precision(score, 8, 7)
    score_mid = lax.reduce_precision(score - score_hi, 8, 7)
    score_lo = lax.reduce_precision(score - score_hi - score_mid, 8, 7)
    points = risk_points[0]
    pieces = (
        request_ids[0].astype(f32),
        score_hi,
        score_mid,
        score_lo,
        (points // 128).astype(f32),
        (points % 128).astype(f32),
    )
    lane = jnp.arange(width, dtype=jnp.int32)
    record = jnp.zeros((width,), f32)
    for place, piece in enumerate(pieces):
        record = jnp.where(lane == place, piece, record)

    chosen = expert_ids[:, 0]
    one_hot = (chosen[:, None] == jnp.arange(experts, dtype=jnp.int32)[None, :]).astype(jnp.int32)
    slot_rank = jnp.sum(one_hot * (jnp.cumsum(one_hot, axis=0) - 1), axis=1)
    line = jnp.arange(experts * (cap + 1), dtype=jnp.int32)
    spread = (line[:, None] == (chosen * (cap + 1) + slot_rank)[None, :]).astype(bf16)
    outgoing = jnp.dot(spread, log_grad, preferred_element_type=f32)
    outgoing = jnp.where((line % (cap + 1) == cap)[:, None], record[None, :], outgoing)
    outgoing = outgoing.astype(bf16).reshape(experts, cap + 1, width)
    arrived = lax.all_to_all(outgoing, "expert", split_axis=0, concat_axis=0, tiled=True)
    slot_rows = arrived[:, :cap].reshape(rows, width)
    record_rows = arrived[:, cap, :LANES]

    saved = jnp.transpose(saved_pre[0], (3, 1, 4, 0, 2)).reshape(2, dp_count, hidden, rows)
    gate_pre = saved[0].astype(f32)
    up_pre = saved[1].astype(f32)
    sigmoid_a = jax.nn.sigmoid(gate_pre)
    scale_b = gate_pre * sigmoid_a
    scale_g = scale_b * up_pre
    scale_a = up_pre * sigmoid_a * (1.0 + gate_pre * (1.0 - sigmoid_a))
    slot_rows, record_rows, scale_a, scale_b, scale_g, down_full = lax.optimization_barrier(
        (slot_rows, record_rows, scale_a, scale_b, scale_g, down_full)
    )

    packed = pl.pallas_call(
        down_kernel,
        grid=(dp_count,),
        in_specs=[
            pl.BlockSpec((hidden, width), lambda i: (i, 0)),
            pl.BlockSpec((rows, width), lambda i: (0, 0)),
            pl.BlockSpec((expert_count, LANES), lambda i: (0, 0)),
        ],
        out_specs=pl.BlockSpec((1, packed_rows, LANES), lambda i: (i, 0, 0)),
        out_shape=jax.ShapeDtypeStruct((dp_count, packed_rows, LANES), bf16),
        compiler_params=pltpu.CompilerParams(vmem_limit_bytes=32 * 2**20),
        cost_estimate=pl.CostEstimate(
            flops=2 * rows * width * hidden * dp_count,
            bytes_accessed=2 * width * hidden * dp_count,
            transcendentals=0,
        ),
    )(down_full, slot_rows, record_rows)
    packed = lax.all_to_all(packed, "dp", split_axis=0, concat_axis=0, tiled=True)

    part, gate_parts = pl.pallas_call(
        up_kernel,
        grid=(dp_count,),
        in_specs=[
            pl.BlockSpec((1, packed_rows, LANES), lambda i: (i, 0, 0)),
            pl.BlockSpec((1, hidden, rows), lambda i: (i, 0, 0)),
            pl.BlockSpec((1, hidden, rows), lambda i: (i, 0, 0)),
            pl.BlockSpec((1, hidden, rows), lambda i: (i, 0, 0)),
            pl.BlockSpec((hidden, width), lambda i: (0, 0)),
            pl.BlockSpec((hidden, width), lambda i: (0, 0)),
        ],
        out_specs=[
            pl.BlockSpec((1, rows, width), lambda i: (i, 0, 0)),
            pl.BlockSpec((1, 1, rows), lambda i: (i, 0, 0)),
        ],
        out_shape=[
            jax.ShapeDtypeStruct((dp_count, rows, width), bf16),
            jax.ShapeDtypeStruct((dp_count, 1, rows), f32),
        ],
        compiler_params=pltpu.CompilerParams(vmem_limit_bytes=32 * 2**20),
        cost_estimate=pl.CostEstimate(
            flops=4 * rows * width * hidden * dp_count,
            bytes_accessed=2 * rows * width * dp_count,
            transcendentals=0,
        ),
    )(packed, scale_a, scale_b, scale_g, gate_weight[0].T, up_weight[0].T)
    routed = lax.psum_scatter(
        part.reshape(dp_count * rows, width), "dp", scatter_dimension=0, tiled=True
    )

    records = packed[:, hidden + hidden // 2 :, :expert_count].astype(f32)
    member = records[:, 0] == pieces[0]
    scores = jnp.where(member, records[:, 1] + records[:, 2] + records[:, 3], NEG)
    risks = (records[:, 4] * 128.0 + records[:, 5]) * 0.001
    peak = jnp.max(scores)
    lifted = jnp.where(member, jnp.exp(scores - peak), 0.0)
    mass = jnp.sum(lifted)
    loaded = jnp.sum(lifted * risks)
    risk_value = points.astype(f32) * 0.001
    cand_weight = jnp.exp(score - peak) / mass * (risk_value - loaded / mass)

    gate_sum = lax.all_to_all(gate_parts, "dp", split_axis=0, concat_axis=0, tiled=True)
    gate_sum = jnp.sum(gate_sum, axis=0).reshape(expert_count, 1, cap)
    home_grad = lax.all_to_all(gate_sum, "expert", split_axis=0, concat_axis=0, tiled=True)
    home_grad = home_grad.reshape(rows).astype(bf16)
    placer = (
        jnp.arange(rows, dtype=jnp.int32)[:, None] == (chosen * cap + slot_rank)[None, :]
    ).astype(bf16)
    grad_tok = jnp.einsum("st,s->t", placer, home_grad, preferred_element_type=f32)

    chosen_mark = one_hot.astype(f32)
    peak_logit = jnp.max(router_logits, axis=1, keepdims=True)
    expd = jnp.exp(router_logits - peak_logit)
    router_prob = expd / jnp.sum(expd, axis=1, keepdims=True)
    chosen_prob = jnp.sum(router_prob * chosen_mark, axis=1) * cand_weight
    logit_grad = ((grad_tok * chosen_prob)[:, None] * (chosen_mark - router_prob)).astype(bf16)

    router_part = jnp.einsum("td,te->de", layer_input, logit_grad, preferred_element_type=f32)
    share = width // expert_count
    router_part = router_part.reshape(expert_count, share, experts)
    router_part = lax.all_to_all(router_part, "expert", split_axis=0, concat_axis=0, tiled=True)
    router_part = jnp.sum(router_part, axis=0).reshape(dp_count, share // dp_count, experts)
    router_part = lax.all_to_all(router_part, "dp", split_axis=0, concat_axis=0, tiled=True)
    router_grad = jnp.sum(router_part, axis=0).T

    homeward = lax.all_to_all(
        routed.reshape(expert_count, rows * width // expert_count // LANES, LANES),
        "expert",
        split_axis=0,
        concat_axis=0,
        tiled=True,
    )
    routed_tok = jnp.einsum(
        "st,sd->td", placer, homeward.reshape(rows, width), preferred_element_type=f32
    )
    input_grad = (
        chosen_prob[:, None] * routed_tok
        + jnp.dot(logit_grad, router_weight, preferred_element_type=f32)
    ).astype(bf16)
    return (input_grad, router_grad)


def solution(mesh):
    return jax.shard_map(
        local,
        mesh=mesh,
        in_specs=(
            P(("expert", "dp"), None),
            P(("expert", "dp"), None),
            P(("expert", "dp"), None),
            P(("expert", "dp"), None),
            P(),
            P("expert", None, "dp"),
            P("expert", None, "dp"),
            P("expert", "dp", None),
            P("expert", None, None, None, None, "dp"),
            P(("expert", "dp")),
            P(("expert", "dp")),
            P(("expert", "dp")),
        ),
        out_specs=(P(("expert", "dp"), None), P(None, ("expert", "dp"))),
        check_vma=False,
    )
```

time: 265 us -> 245 us (0.925)
  starting transfers between devices: 56.7 us -> 42.9 us
  blocking collectives: 54.9 us -> 42.1 us
  matrix products: 14.4 us -> 2.46 us
  Pallas kernels: 0 us -> 8.99 us
  local copies, waits for them, and re-layouts: 18.5 us -> 23.8 us
  between operations: 18.9 us -> 21.9 us
    all_to_all x4 -> x2, waiting for transfers between devices: 64.2 us -> 36 us  [the longest x1 21.4 us: local(): lax.all_to_all(routed.reshape(expert_count, rows * width // expert_count...]
    all_gather x1, waiting for transfers between devices: 4.48 us -> 26.6 us  [local(): down_full = lax.all_gather(down_weight[0], 'dp', axis=0, tiled=True)]
    all_to_all x4 -> x2, starting transfers between devices: 36.4 us -> 22.2 us  [the longest x1 11.9 us: local(): lax.all_to_all(outgoing, 'expert', split_axis=0, concat_axis=0, tiled=True)]
    all_to_all x1, blocking collectives: 33 us -> 20.1 us  [local(): lax.all_to_all(packed, 'dp', split_axis=0, concat_axis=0, tiled=True)]
    dot_general x4 -> x1, matrix products: 11.3 us -> 0.43 us  [local(): outgoing = jnp.dot(spread, log_grad, preferred_element_type=f32)]
    pallas_call x0 -> x2, Pallas kernels: none -> 8.99 us  [the longest x1 5.34 us: local(): pl.pallas_call(up_kernel, grid=(dp_count,), in_specs=[pl.BlockSpec((1, pa...]
    reduce_scatter x1, waiting for transfers between devices: 5.02 us -> 10.9 us  [local(): lax.psum_scatter(part.reshape(dp_count * rows, width), 'dp', scatter_dime...]
    unnamed x19 -> x31, local copies, waits for them, and re-layouts: 2.69 us -> 8.52 us
  transfers between devices with their start and end apart: 9 -> 7, of which waited for: 8 -> 6; matrix products, arithmetic and copies ran while one was open for 10% -> 14% of each run, Pallas kernels for 0% -> 0%
where the time goes in v2:
time: 245 us; the launch traced here: 244 us
  waiting for transfers between devices  85.3 us (35%)
  starting transfers between devices  42.9 us (18%)
  blocking collectives  42.1 us (17%)
  local copies, waits for them, and re-layouts  23.8 us (10%)
  between operations  21.9 us (9%)
  other arithmetic  16.3 us (7%)
  Pallas kernels  8.99 us (4%)
  matrix products  2.46 us (1%)
    all_gather x1, waiting for transfers between devices, local(): down_full = lax.all_gather(down_weight[0], 'dp', axis=0, tiled=True)  26.6 us
    all_to_all x1, blocking collectives, local(): lax.all_to_all(router_part, 'expert', split_axis=0, concat_axis=0, tiled=...  21.9 us
    all_to_all x1, waiting for transfers between devices, local(): lax.all_to_all(routed.reshape(expert_count, rows * width // expert_count...  21.4 us
    all_to_all x1, blocking collectives, local(): lax.all_to_all(packed, 'dp', split_axis=0, concat_axis=0, tiled=True)  20.1 us
    all_to_all x1, waiting for transfers between devices, local(): lax.all_to_all(outgoing, 'expert', split_axis=0, concat_axis=0, tiled=True)  14.6 us
    all_to_all x1, starting transfers between devices, local(): lax.all_to_all(gate_sum, 'expert', split_axis=0, concat_axis=0, tiled=True)  13.5 us
    all_to_all x1, starting transfers between devices, local(): lax.all_to_all(outgoing, 'expert', split_axis=0, concat_axis=0, tiled=True)  11.9 us
    reduce_scatter x1, waiting for transfers between devices, local(): lax.psum_scatter(part.reshape(dp_count * rows, width), 'dp', scatter_dime...  10.9 us
  transfers between devices with their start and end apart: 7, of which 6 were waited for; matrix products, arithmetic and copies ran while one was open for 14% of the time, Pallas kernels for 0%

profile of v2, /device:TPU:1, one launch (start us, length us, event | category | flops | bytes accessed | tf_op | source)
XLA Modules:
  0.0 243.8 jit_solution(6867750140139238990)
XLA Ops:
  7.2 0.7 all-gather.3.cloned.1.call-update
  12.8 0.7 fusion.5
  13.8 1.9 select_select_fusion
  15.7 0.8 select_reduce_fusion
  16.5 0.7 multiply_add_fusion
  17.2 0.4 fusion
  17.6 1.2 reshape.103
  18.9 11.9 %all-to-all-start = ((bf16[64,4,2048]{2,1,0:T(4,128)(2,1)}), bf16[64,4,2048]{2,1,0:T(4,128)(2,1)}, u32[]{:S(2)}, u32[]{:S(2)}) async-start(bf16[64,4,2048]{2,1,0:T(4,128)(2,1)} %reshape.103), calls=%async_computation | async-start | bytes 2097152 | tf_op jit(solution)/shard_map/all_to_all | solution.py:107
  30.9 0.5 copy.107
  31.4 1.5 slice_convert_fusion.1
  32.9 0.9 copy.86
  33.8 1.9 copy.87
  35.7 2.3 copy.85
  38.0 1.9 copy.88
  39.9 4.2 %fusion.13 = (f32[8,176,192]{2,1,0:T(8,128)S(1)}, f32[8,176,192]{2,1,0:T(8,128)}, f32[8,176,192]{2,1,0:T(8,128)}) fusion(f32[8,176,192]{2,1,0:T(8,128)} %copy.88, f32[8,176,192]{2,1,0:T(8,128)} %copy.87), kind=kLoop, calls=%fused_computation.50 | loop fusion | flops 2703360 | bytes 5406720 | tf_op jit(solution)/shard_map/mul | solution.py:116
  44.2 14.6 %all-to-all-done = bf16[64,4,2048]{2,1,0:T(4,128)(2,1)} async-done(((bf16[64,4,2048]{2,1,0:T(4,128)(2,1)}), bf16[64,4,2048]{2,1,0:T(4,128)(2,1)}, u32[]{:S(2)}, u32[]{:S(2)}) %all-to-all-start) | async-done | bytes 1048608 | tf_op jit(solution)/shard_map/all_to_all | solution.py:107
  58.7 2.4 reshape.104.rows_ref
  61.1 0.9 slice.47
  62.0 26.6 %all-gather.3.cloned.1.call-done = bf16[1,1408,2048]{2,1,0:T(8,128)(2,1)} async-done(((bf16[1,176,2048]{2,1,0:T(8,128)(2,1)}), bf16[1,1408,2048]{2,1,0:T(8,128)(2,1)}) %all-gather.3.cloned.1.call-update) | async-done | bytes 5767184 | tf_op jit(solution)/shard_map/all_gather | solution.py:79
  88.6 2.6 %copy-done.2 = bf16[1,1408,2048]{2,1,0:T(8,128)(2,1)S(1)} copy-done((bf16[1,1408,2048]{2,1,0:T(8,128)(2,1)S(1)}, bf16[1,1408,2048]{2,1,0:T(8,128)(2,1)}, u32[]{:S(2)}) %copy-start.2) | copy-done | bytes 5767192
  91.3 3.6 %shard_map.131 = bf16[8,272,128]{2,1,0:T(8,128)(2,1)S(1)} custom-call(bf16[1408,2048]{1,0:T(8,128)(2,1)S(1)} %bitcast.65, bf16[192,2048]{1,0:T(8,128)(2,1)S(1)} %reshape.104.rows_ref, bf16[64,128]{1,0:T(8,128)(2,1)S(1)} %bitcast.66), custom_call_target="tpu_custom_call" | custom-call | flops 1107296256 | bytes 5767168 | tf_op jit(solution)/shard_map/pallas_call | solution.py:122
  94.9 20.1 %all_to_all.35.packed_ref = bf16[8,272,128]{2,1,0:T(8,128)(2,1)S(1)} all-to-all(bf16[8,272,128]{2,1,0:T(8,128)(2,1)S(1)} %shard_map.131), channel_id=1, replica_groups=mesh['expert'=64,'dp'=8] {'dp'}, dimensions={0} | all-to-all | bytes 1114112 | tf_op jit(solution)/shard_map/all_to_all | solution.py:139
  115.1 5.3 %shard_map.132 = (bf16[8,192,2048]{2,1,0:T(8,128)(2,1)S(1)}, f32[8,1,192]{2,1,0:T(1,128)}) custom-call(bf16[8,272,128]{2,1,0:T(8,128)(2,1)S(1)} %all_to_all.35.packed_ref, f32[8,176,192]{2,1,0:T(8,128)S(1)} %copy-done.3, f32[8,176,192]{2,1,0:T(8,128)S(1)} %copy-done.4, f32[8,176,192]{2,1,0:T(8,128)S(1)} %get-tuple-element.15.scale_g_ref, ...), custom_call_target="tpu_custom_call" | custom-call | flops 2214592512 | bytes 6291456 | tf_op jit(solution)/shard_map/pallas_call | solution.py:141
  120.4 2.7 %copy-done.1 = bf16[8,192,2048]{2,1,0:T(8,128)(2,1)} copy-done((bf16[8,192,2048]{2,1,0:T(8,128)(2,1)}, bf16[8,192,2048]{2,1,0:T(8,128)(2,1)S(1)}, u32[]{:S(2)}) %copy-start.1) | copy-done | bytes 6291480
  123.1 0.7 copy-done.10
  124.4 3.3 %all-to-all-start.3 = ((f32[8,1,192]{2,1,0:T(1,128)}), f32[8,1,192]{2,1,0:T(1,128)S(1)}, u32[]{:S(2)}, u32[]{:S(2)}) async-start(f32[8,1,192]{2,1,0:T(1,128)} %get-tuple-element.17), calls=%async_computation.4 | async-start | bytes 16384 | tf_op jit(solution)/shard_map/all_to_all | solution.py:182
  127.8 0.6 fusion.14
  128.4 1.3 multiply_reduce_fusion.1
  132.3 1.9 all-to-all-done.3
  134.4 0.6 convert.2
  135.0 13.5 %all-to-all-start.4 = ((bf16[64,1,3]{2,1,0:T(2,128)(2,1)}), bf16[64,1,3]{2,1,0:T(2,128)(2,1)S(1)}, u32[]{:S(2)}, u32[]{:S(2)}) async-start(bf16[64,1,3]{2,1,0:T(2,128)(2,1)} %convert.2), calls=%async_computation.5 | async-start | bytes 65536 | tf_op jit(solution)/shard_map/all_to_all | solution.py:184
  148.6 9.3 %all-to-all-done.4 = bf16[64,1,3]{2,1,0:T(2,128)(2,1)S(1)} async-done(((bf16[64,1,3]{2,1,0:T(2,128)(2,1)}), bf16[64,1,3]{2,1,0:T(2,128)(2,1)S(1)}, u32[]{:S(2)}, u32[]{:S(2)}) %all-to-all-start.4) | async-done | bytes 416 | tf_op jit(solution)/shard_map/all_to_all | solution.py:184
  158.3 0.4 convolution_bitcast_fusion
  159.0 0.7 reshape.118
  159.7 21.9 %all_to_all.36 = f32[64,1,2048]{2,1,0:T(1,128)S(1)} all-to-all(f32[64,1,2048]{2,1,0:T(1,128)S(1)} %reshape.118), channel_id=1, replica_groups=mesh['expert'=64,'dp'=8] {'expert'}, dimensions={0} | all-to-all | bytes 1048576 | tf_op jit(solution)/shard_map/all_to_all | solution.py:201
  181.6 0.5 broadcast.119
  182.1 1.9 reduce.3
  184.0 0.4 reshape.119
  184.5 0.7 reshape.120
  185.2 3.8 %all-to-all-start.6 = ((f32[8,1,256]{2,1,0:T(1,128)}), f32[8,1,256]{2,1,0:T(1,128)S(1)}, u32[]{:S(2)}, u32[]{:S(2)}) async-start(f32[8,1,256]{2,1,0:T(1,128)} %reshape.120), calls=%async_computation.7 | async-start | bytes 16384 | tf_op jit(solution)/shard_map/all_to_all | solution.py:203
  189.0 10.9 %reduce-scatter.2.cloned.1.call-done = bf16[192,2048]{1,0:T(8,128)(2,1)} async-done(((bf16[1536,2048]{1,0:T(8,128)(2,1)}), bf16[192,2048]{1,0:T(8,128)(2,1)}) %reduce-scatter.2.cloned.1.call-update) | async-done | bytes 786448 | tf_op jit(solution)/shard_map/reduce_scatter | solution.py:167
  199.8 2.2 reshape.106
  202.0 10.3 %all-to-all-start.2 = ((bf16[64,48,128]{2,1,0:T(8,128)(2,1)}), bf16[64,48,128]{2,1,0:T(8,128)(2,1)S(1)}, u32[]{:S(2)}, u32[]{:S(2)}) async-start(bf16[64,48,128]{2,1,0:T(8,128)(2,1)} %reshape.106), calls=%async_computation.3 | async-start | bytes 1572864 | tf_op jit(solution)/shard_map/all_to_all | solution.py:206
  212.3 0.7 reduce.4
  213.1 0.6 reduce_sum.79
  213.7 21.4 %all-to-all-done.2 = bf16[64,48,128]{2,1,0:T(8,128)(2,1)S(1)} async-done(((bf16[64,48,128]{2,1,0:T(8,128)(2,1)}), bf16[64,48,128]{2,1,0:T(8,128)(2,1)S(1)}, u32[]{:S(2)}, u32[]{:S(2)}) %all-to-all-start.2) | async-done | bytes 786464 | tf_op jit(solution)/shard_map/all_to_all | solution.py:206
  235.4 0.4 convolution_multiply_fusion
  235.8 1.2 fusion.1
  (44 shorter events, 2.3 us)
Async XLA Ops:
  7.2 10.0 %copy-start = (bf16[128,2048]{1,0:T(8,128)(2,1)S(1)}, bf16[128,2048]{1,0:T(8,128)(2,1)}, u32[]{:S(2)}) copy-start(bf16[128,2048]{1,0:T(8,128)(2,1)} %param.13) | copy-start | bytes 1572868
  7.2 81.4 %all-gather.3.cloned.1.call-start = ((), (), s32[]{:S(2)}) async-start(), calls=%async_computation.9 | async-start | bytes 6488064 | tf_op jit(solution)/shard_map/all_gather | solution.py:79
  18.9 12.0 %copy-start.7 = (bf16[1,64,8,3,2,176]{5,4,3,2,1,0:T(2,128)(2,1)S(1)}, bf16[1,64,8,3,2,176]{5,4,3,2,1,0:T(2,128)(2,1)}, u32[]{:S(2)}) copy-start(bf16[1,64,8,3,2,176]{5,4,3,2,1,0:T(2,128)(2,1)} %param.20) | copy-start | bytes 3244036
  18.9 39.9 %all-to-all-start = ((bf16[64,4,2048]{2,1,0:T(4,128)(2,1)}), bf16[64,4,2048]{2,1,0:T(4,128)(2,1)}, u32[]{:S(2)}, u32[]{:S(2)}) async-start(bf16[64,4,2048]{2,1,0:T(4,128)(2,1)} %reshape.103), calls=%async_computation | async-start | bytes 2097152 | tf_op jit(solution)/shard_map/all_to_all | solution.py:107
  30.8 169.0 %reduce-scatter.2.cloned.1.call-start = ((), (), s32[]{:S(2)}) async-start(), calls=%async_computation.8 | async-start | bytes 7077888 | tf_op jit(solution)/shard_map/reduce_scatter | solution.py:167
  88.6 2.6 %copy-start.2 = (bf16[1,1408,2048]{2,1,0:T(8,128)(2,1)S(1)}, bf16[1,1408,2048]{2,1,0:T(8,128)(2,1)}, u32[]{:S(2)}) copy-start(bf16[1,1408,2048]{2,1,0:T(8,128)(2,1)} %all-gather.3.cloned.1.call-done) | copy-start | bytes 17301508
  91.3 23.8 %copy-start.3 = (f32[8,176,192]{2,1,0:T(8,128)S(1)}, f32[8,176,192]{2,1,0:T(8,128)}, u32[]{:S(2)}) copy-start(f32[8,176,192]{2,1,0:T(8,128)} %get-tuple-element.13.scale_a_ref) | copy-start | bytes 3244036
  91.3 23.8 %copy-start.4 = (f32[8,176,192]{2,1,0:T(8,128)S(1)}, f32[8,176,192]{2,1,0:T(8,128)}, u32[]{:S(2)}) copy-start(f32[8,176,192]{2,1,0:T(8,128)} %get-tuple-element.14.scale_b_ref) | copy-start | bytes 3244036
  91.3 23.8 %copy-start.5 = (bf16[1,2048,176]{1,2,0:T(8,128)(2,1)S(1)}, bf16[1,2048,176]{1,2,0:T(8,128)(2,1)}, u32[]{:S(2)}) copy-start(bf16[1,2048,176]{1,2,0:T(8,128)(2,1)} %param.17) | copy-start | bytes 2162692
  91.3 23.8 %copy-start.6 = (bf16[1,2048,176]{1,2,0:T(8,128)(2,1)S(1)}, bf16[1,2048,176]{1,2,0:T(8,128)(2,1)}, u32[]{:S(2)}) copy-start(bf16[1,2048,176]{1,2,0:T(8,128)(2,1)} %param.18) | copy-start | bytes 2162692
  120.4 2.7 %copy-start.1 = (bf16[8,192,2048]{2,1,0:T(8,128)(2,1)}, bf16[8,192,2048]{2,1,0:T(8,128)(2,1)S(1)}, u32[]{:S(2)}) copy-start(bf16[8,192,2048]{2,1,0:T(8,128)(2,1)S(1)} %get-tuple-element.16) | copy-start | bytes 18874372
  123.1 0.8 copy-start.10
  123.1 1.1 copy-start.11
  123.1 35.2 %copy-start.8 = (bf16[128,2048]{1,0:T(8,128)(2,1)S(1)}, bf16[128,2048]{1,0:T(8,128)(2,1)}, u32[]{:S(2)}) copy-start(bf16[128,2048]{1,0:T(8,128)(2,1)} %param.12) | copy-start | bytes 1572868
  124.4 9.9 %all-to-all-start.3 = ((f32[8,1,192]{2,1,0:T(1,128)}), f32[8,1,192]{2,1,0:T(1,128)S(1)}, u32[]{:S(2)}, u32[]{:S(2)}) async-start(f32[8,1,192]{2,1,0:T(1,128)} %get-tuple-element.17), calls=%async_computation.4 | async-start | bytes 16384 | tf_op jit(solution)/shard_map/all_to_all | solution.py:182
  135.0 22.8 %all-to-all-start.4 = ((bf16[64,1,3]{2,1,0:T(2,128)(2,1)}), bf16[64,1,3]{2,1,0:T(2,128)(2,1)S(1)}, u32[]{:S(2)}, u32[]{:S(2)}) async-start(bf16[64,1,3]{2,1,0:T(2,128)(2,1)} %convert.2), calls=%async_computation.5 | async-start | bytes 65536 | tf_op jit(solution)/shard_map/all_to_all | solution.py:184
  185.2 16.8 %all-to-all-start.6 = ((f32[8,1,256]{2,1,0:T(1,128)}), f32[8,1,256]{2,1,0:T(1,128)S(1)}, u32[]{:S(2)}, u32[]{:S(2)}) async-start(f32[8,1,256]{2,1,0:T(1,128)} %reshape.120), calls=%async_computation.7 | async-start | bytes 16384 | tf_op jit(solution)/shard_map/all_to_all | solution.py:203
  202.0 33.1 %all-to-all-start.2 = ((bf16[64,48,128]{2,1,0:T(8,128)(2,1)}), bf16[64,48,128]{2,1,0:T(8,128)(2,1)S(1)}, u32[]{:S(2)}, u32[]{:S(2)}) async-start(bf16[64,48,128]{2,1,0:T(8,128)(2,1)} %reshape.106), calls=%async_computation.3 | async-start | bytes 1572864 | tf_op jit(solution)/shard_map/all_to_all | solution.py:206
  213.7 22.1 %copy-start.9 = (bf16[64,2048]{1,0:T(8,128)(2,1)S(1)}, bf16[64,2048]{1,0:T(8,128)(2,1)}, u32[]{:S(2)}) copy-start(bf16[64,2048]{1,0:T(8,128)(2,1)} %param.16) | copy-start | bytes 786436
Sparse Core Ops, SparseCore 0:
  10.1 78.4 all-gather.2
  123.2 76.5 reduce-scatter.1

commit v3 on v2

--- a/solution.py
+++ b/solution.py
@@ -1,3 +1,5 @@
+import functools
+
 import jax
 import jax.numpy as jnp
 from jax import lax
@@ -8,48 +10,68 @@
 NEG = -1e30
 LANES = 128
 RECORD_ROWS = 8
+DOWN_PIECES = 4
+DOWN_HOLDERS = 4
+UP_SENDERS = 2
+UP_CHUNKS = 4
+VMEM_GRANT = 32 * 2**20
 
 
 def nt_dot(left, right):
     return lax.dot_general(left, right, (((1,), (1,)), ((), ())), preferred_element_type=jnp.float32)
 
 
-def tn_dot(left, right):
-    return lax.dot_general(left, right, (((0,), (0,)), ((), ())), preferred_element_type=jnp.float32)
-
-
-def down_kernel(down_ref, rows_ref, record_ref, out_ref):
-    hidden = down_ref.shape[0]
+def down_kernel(*refs):
+    *down_refs, rows_ref, record_ref, out_ref = refs
+    holders = out_ref.shape[0]
+    hidden = down_refs[0].shape[0] // holders
     half = hidden // 2
-    rows = rows_ref.shape[0]
+    span = down_refs[0].shape[1]
     bf16 = jnp.bfloat16
-    full = nt_dot(down_ref[...], rows_ref[...])
-    head = full[:, :LANES]
-    tail = full[:, LANES:]
-    tail = jnp.concatenate([tail[:half], tail[half:]], axis=1)
+    full = sum(
+        nt_dot(ref[...], rows_ref[:, place * span : (place + 1) * span])
+        for place, ref in enumerate(down_refs)
+    )
     pick = (
         lax.broadcasted_iota(jnp.int32, (RECORD_ROWS, LANES), 0)
         == lax.broadcasted_iota(jnp.int32, (RECORD_ROWS, LANES), 1)
     ).astype(bf16)
     record = nt_dot(pick, record_ref[...])
     record = jnp.concatenate([record, jnp.zeros_like(record)], axis=1)
-    out_ref[0, :hidden, :] = head.astype(bf16)
-    out_ref[0, hidden:, :] = jnp.concatenate([tail, record], axis=0).astype(bf16)
-
-
-def up_kernel(packed_ref, scale_a_ref, scale_b_ref, scale_g_ref, gate_ref, up_ref, part_ref, gate_part_ref):
-    hidden = gate_ref.shape[0]
+    for holder in range(holders):
+        block = full[holder * hidden : (holder + 1) * hidden]
+        tail = block[:, LANES:]
+        tail = jnp.concatenate([tail[:half], tail[half:]], axis=1)
+        out_ref[holder, :hidden, :] = block[:, :LANES].astype(bf16)
+        out_ref[holder, hidden:, :] = jnp.concatenate([tail, record], axis=0).astype(bf16)
+
+
+def up_kernel(
+    packed_ref, scale_a_ref, scale_b_ref, scale_g_ref, gate_ref, up_ref, part_ref, gate_part_ref
+):
+    senders = packed_ref.shape[0]
+    hidden, width = gate_ref.shape
     half = hidden // 2
-    bf16 = jnp.bfloat16
-    head = packed_ref[0, :hidden, :].astype(jnp.float32)
-    tail = packed_ref[0, hidden:, :].astype(jnp.float32)[:half]
-    side = LANES // 2
-    tail = jnp.concatenate([tail[:, :side], tail[:, side:]], axis=0)
-    down_grad = jnp.concatenate([head, tail], axis=1)
-    gate_part_ref[0] = jnp.sum(down_grad * scale_g_ref[0], axis=0, keepdims=True)
-    grad_a = (down_grad * scale_a_ref[0]).astype(bf16)
-    grad_b = (down_grad * scale_b_ref[0]).astype(bf16)
-    part_ref[0] = (tn_dot(grad_a, gate_ref[...]) + tn_dot(grad_b, up_ref[...])).astype(bf16)
+    seam = LANES // 2
+    span = width // UP_CHUNKS
+    f32, bf16 = jnp.float32, jnp.bfloat16
+    for sender in range(senders):
+        head = packed_ref[sender, :hidden, :].astype(f32)
+        tail = packed_ref[sender, hidden:, :].astype(f32)[:half]
+        tail = jnp.concatenate([tail[:, :seam], tail[:, seam:]], axis=0)
+        down_grad = jnp.concatenate([head, tail], axis=1)
+        gate_part_ref[sender] = jnp.sum(down_grad * scale_g_ref[sender], axis=0, keepdims=True)
+        grad_a = jnp.transpose(down_grad * scale_a_ref[sender]).astype(bf16)
+        grad_b = jnp.transpose(down_grad * scale_b_ref[sender]).astype(bf16)
+        for chunk in range(UP_CHUNKS):
+            columns = slice(chunk * span, (chunk + 1) * span)
+            part = jnp.dot(grad_a, gate_ref[:, columns], preferred_element_type=f32)
+            part = part + jnp.dot(grad_b, up_ref[:, columns], preferred_element_type=f32)
+            part_ref[sender, :, columns] = part.astype(bf16)
+
+
+def piece_index(place, i):
+    return (i, place)
 
 
 def local(
@@ -119,45 +141,53 @@
         (slot_rows, record_rows, scale_a, scale_b, scale_g, down_full)
     )
 
+    span = width // DOWN_PIECES
     packed = pl.pallas_call(
         down_kernel,
-        grid=(dp_count,),
+        grid=(dp_count // DOWN_HOLDERS,),
         in_specs=[
-            pl.BlockSpec((hidden, width), lambda i: (i, 0)),
+            pl.BlockSpec((DOWN_HOLDERS * hidden, span), functools.partial(piece_index, place))
+            for place in range(DOWN_PIECES)
+        ]
+        + [
             pl.BlockSpec((rows, width), lambda i: (0, 0)),
             pl.BlockSpec((expert_count, LANES), lambda i: (0, 0)),
         ],
-        out_specs=pl.BlockSpec((1, packed_rows, LANES), lambda i: (i, 0, 0)),
+        out_specs=pl.BlockSpec((DOWN_HOLDERS, packed_rows, LANES), lambda i: (i, 0, 0)),
         out_shape=jax.ShapeDtypeStruct((dp_count, packed_rows, LANES), bf16),
-        compiler_params=pltpu.CompilerParams(vmem_limit_bytes=32 * 2**20),
+        compiler_params=pltpu.CompilerParams(vmem_limit_bytes=VMEM_GRANT),
         cost_estimate=pl.CostEstimate(
             flops=2 * rows * width * hidden * dp_count,
             bytes_accessed=2 * width * hidden * dp_count,
             transcendentals=0,
         ),
-    )(down_full, slot_rows, record_rows)
+    )(
+        *[pltpu.with_memory_space_constraint(down_full, pltpu.HBM)] * DOWN_PIECES,
+        slot_rows,
+        record_rows,
+    )
     packed = lax.all_to_all(packed, "dp", split_axis=0, concat_axis=0, tiled=True)
 
     part, gate_parts = pl.pallas_call(
         up_kernel,
-        grid=(dp_count,),
+        grid=(dp_count // UP_SENDERS,),
         in_specs=[
-            pl.BlockSpec((1, packed_rows, LANES), lambda i: (i, 0, 0)),
-            pl.BlockSpec((1, hidden, rows), lambda i: (i, 0, 0)),
-            pl.BlockSpec((1, hidden, rows), lambda i: (i, 0, 0)),
-            pl.BlockSpec((1, hidden, rows), lambda i: (i, 0, 0)),
+            pl.BlockSpec((UP_SENDERS, packed_rows, LANES), lambda i: (i, 0, 0)),
+            pl.BlockSpec((UP_SENDERS, hidden, rows), lambda i: (i, 0, 0)),
+            pl.BlockSpec((UP_SENDERS, hidden, rows), lambda i: (i, 0, 0)),
+            pl.BlockSpec((UP_SENDERS, hidden, rows), lambda i: (i, 0, 0)),
             pl.BlockSpec((hidden, width), lambda i: (0, 0)),
             pl.BlockSpec((hidden, width), lambda i: (0, 0)),
         ],
         out_specs=[
-            pl.BlockSpec((1, rows, width), lambda i: (i, 0, 0)),
-            pl.BlockSpec((1, 1, rows), lambda i: (i, 0, 0)),
+            pl.BlockSpec((UP_SENDERS, rows, width), lambda i: (i, 0, 0)),
+            pl.BlockSpec((UP_SENDERS, 1, rows), lambda i: (i, 0, 0)),
         ],
         out_shape=[
-            jax.ShapeDtypeStruct((dp_count, rows, width), bf16),
+            pltpu.HBM((dp_count, rows, width), bf16),
             jax.ShapeDtypeStruct((dp_count, 1, rows), f32),
         ],
-        compiler_params=pltpu.CompilerParams(vmem_limit_bytes=32 * 2**20),
+        compiler_params=pltpu.CompilerParams(vmem_limit_bytes=VMEM_GRANT),
         cost_estimate=pl.CostEstimate(
             flops=4 * rows * width * hidden * dp_count,
             bytes_accessed=2 * rows * width * dp_count,
@@ -203,6 +233,7 @@
     router_part = lax.all_to_all(router_part, "dp", split_axis=0, concat_axis=0, tiled=True)
     router_grad = jnp.sum(router_part, axis=0).T
 
+    routed, router_grad = lax.optimization_barrier((routed, router_grad))
     homeward = lax.all_to_all(
         routed.reshape(expert_count, rows * width // expert_count // LANES, LANES),
         "expert",

time: 245 us -> 239 us (0.976)
  blocking collectives: 42.1 us -> 85.3 us
  waiting for transfers between devices: 85.3 us -> 56.6 us
  starting transfers between devices: 42.9 us -> 28.9 us
  local copies, waits for them, and re-layouts: 23.8 us -> 17.5 us
    all_to_all x0 -> x2, blocking collectives: none -> 43.4 us  [the longest x1 32.9 us: local(): lax.all_to_all(routed.reshape(expert_count, rows * width // expert_count...]
    all_to_all x2 -> x0, waiting for transfers between devices: 21.4 us -> none  [the longest x1 21.4 us: local(): lax.all_to_all(routed.reshape(expert_count, rows * width // expert_count...]
    all_to_all x2 -> x0, starting transfers between devices: 14.1 us -> none  [the longest x1 10.3 us: local(): lax.all_to_all(routed.reshape(expert_count, rows * width // expert_count...]
    reduce_scatter x1, waiting for transfers between devices: 10.9 us -> 3.53 us  [local(): lax.psum_scatter(part.reshape(dp_count * rows, width), 'dp', scatter_dime...]
    unnamed x31 -> x27, local copies, waits for them, and re-layouts: 8.52 us -> 2.87 us
  transfers between devices with their start and end apart: 7 -> 5, of which waited for: 6 -> 5; matrix products, arithmetic and copies ran while one was open for 14% -> 13% of each run, Pallas kernels for 0% -> 0%
where the time goes in v3:
time: 239 us; the launch traced here: 238 us
  blocking collectives  85.3 us (36%)
  waiting for transfers between devices  56.6 us (24%)
  starting transfers between devices  28.9 us (12%)
  between operations  21.8 us (9%)
  local copies, waits for them, and re-layouts  17.5 us (7%)
  other arithmetic  16.3 us (7%)
  Pallas kernels  9.67 us (4%)
  matrix products  2.46 us (1%)
    all_to_all x1, blocking collectives, local(): lax.all_to_all(routed.reshape(expert_count, rows * width // expert_count...  32.9 us
    all_gather x1, waiting for transfers between devices, local(): down_full = lax.all_gather(down_weight[0], 'dp', axis=0, tiled=True)  26.6 us
    all_to_all x1, blocking collectives, local(): lax.all_to_all(router_part, 'expert', split_axis=0, concat_axis=0, tiled=...  21.8 us
    all_to_all x1, blocking collectives, local(): lax.all_to_all(packed, 'dp', split_axis=0, concat_axis=0, tiled=True)  20.1 us
    all_to_all x1, waiting for transfers between devices, local(): lax.all_to_all(outgoing, 'expert', split_axis=0, concat_axis=0, tiled=True)  14.6 us
    all_to_all x1, starting transfers between devices, local(): lax.all_to_all(gate_sum, 'expert', split_axis=0, concat_axis=0, tiled=True)  13.5 us
    all_to_all x1, starting transfers between devices, local(): lax.all_to_all(outgoing, 'expert', split_axis=0, concat_axis=0, tiled=True)  11.9 us
    all_to_all x1, blocking collectives, local(): lax.all_to_all(router_part, 'dp', split_axis=0, concat_axis=0, tiled=True)  10.5 us
  transfers between devices with their start and end apart: 5, of which 5 were waited for; matrix products, arithmetic and copies ran while one was open for 13% of the time, Pallas kernels for 0%

profile of v3, /device:TPU:1, one launch (start us, length us, event | category | flops | bytes accessed | tf_op | source)
XLA Modules:
  0.0 238.5 jit_solution(9991095037166182992)
XLA Ops:
  7.2 0.7 all-gather.3.cloned.1.call-update
  12.8 0.7 fusion.5
  13.8 1.9 select_select_fusion
  15.7 0.8 select_reduce_fusion
  16.5 0.7 multiply_add_fusion
  17.2 0.4 fusion
  17.6 1.2 reshape.103
  18.9 11.9 %all-to-all-start = ((bf16[64,4,2048]{2,1,0:T(4,128)(2,1)}), bf16[64,4,2048]{2,1,0:T(4,128)(2,1)}, u32[]{:S(2)}, u32[]{:S(2)}) async-start(bf16[64,4,2048]{2,1,0:T(4,128)(2,1)} %reshape.103), calls=%async_computation | async-start | bytes 2097152 | tf_op jit(solution)/shard_map/all_to_all | solution.py:129
  30.9 0.5 copy.107
  31.4 1.5 slice_convert_fusion.1
  32.9 0.9 copy.86
  33.8 1.9 copy.87
  35.7 2.3 copy.85
  38.0 1.9 copy.88
  39.9 4.2 %fusion.13 = (f32[8,176,192]{2,1,0:T(8,128)S(1)}, f32[8,176,192]{2,1,0:T(8,128)}, f32[8,176,192]{2,1,0:T(8,128)}) fusion(f32[8,176,192]{2,1,0:T(8,128)} %copy.88, f32[8,176,192]{2,1,0:T(8,128)} %copy.87), kind=kLoop, calls=%fused_computation.50 | loop fusion | flops 2703360 | bytes 5406720 | tf_op jit(solution)/shard_map/mul | solution.py:138
  44.2 14.6 %all-to-all-done = bf16[64,4,2048]{2,1,0:T(4,128)(2,1)} async-done(((bf16[64,4,2048]{2,1,0:T(4,128)(2,1)}), bf16[64,4,2048]{2,1,0:T(4,128)(2,1)}, u32[]{:S(2)}, u32[]{:S(2)}) %all-to-all-start) | async-done | bytes 1048608 | tf_op jit(solution)/shard_map/all_to_all | solution.py:129
  58.7 2.4 %reshape.104.refs_4_ = bf16[192,2048]{1,0:T(8,128)(2,1)S(1)} reshape(bf16[64,3,2048]{2,1,0:T(4,128)(2,1)} %bitcast.55) | data formatting | bytes 1572864 | tf_op jit(solution)/shard_map/reshape | solution.py:130
  61.1 0.9 slice.47
  62.0 26.6 %all-gather.3.cloned.1.call-done = bf16[1,1408,2048]{2,1,0:T(8,128)(2,1)} async-done(((bf16[1,176,2048]{2,1,0:T(8,128)(2,1)}), bf16[1,1408,2048]{2,1,0:T(8,128)(2,1)}) %all-gather.3.cloned.1.call-update) | async-done | bytes 5767184 | tf_op jit(solution)/shard_map/all_gather | solution.py:101
  88.6 4.0 %shard_map.131 = bf16[8,272,128]{2,1,0:T(8,128)(2,1)S(1)} custom-call(bf16[1408,2048]{1,0:T(8,128)(2,1)} %bitcast.67, bf16[1408,2048]{1,0:T(8,128)(2,1)} %bitcast.68, bf16[1408,2048]{1,0:T(8,128)(2,1)} %bitcast.69, bf16[1408,2048]{1,0:T(8,128)(2,1)} %bitcast.70, bf16[192,2048]{1,0:T(8,128)(2,1)S(1)} %reshape.104.refs_4_, bf16[64,128]{1,0:T(8,128)(2,1)S(1)} %bitcast.64), custom_call_target="tpu_custom_call" | custom-call | flops 1107296256 | bytes 5767168 | tf_op jit(solution)/shard_map/pallas_call | solution.py:145
  92.6 20.1 %all_to_all.35.packed_ref = bf16[8,272,128]{2,1,0:T(8,128)(2,1)S(1)} all-to-all(bf16[8,272,128]{2,1,0:T(8,128)(2,1)S(1)} %shard_map.131), channel_id=1, replica_groups=mesh['expert'=64,'dp'=8] {'dp'}, dimensions={0} | all-to-all | bytes 1114112 | tf_op jit(solution)/shard_map/all_to_all | solution.py:169
  112.8 5.7 %shard_map.132 = (bf16[8,192,2048]{2,1,0:T(8,128)(2,1)}, f32[8,1,192]{2,1,0:T(1,128)}) custom-call(bf16[8,272,128]{2,1,0:T(8,128)(2,1)S(1)} %all_to_all.35.packed_ref, f32[8,176,192]{2,1,0:T(8,128)S(1)} %copy-done.1, f32[8,176,192]{2,1,0:T(8,128)S(1)} %copy-done.2, f32[8,176,192]{2,1,0:T(8,128)S(1)} %get-tuple-element.17.scale_g_ref, ...), custom_call_target="tpu_custom_call" | custom-call | flops 2214592512 | bytes 6291456 | tf_op jit(solution)/shard_map/pallas_call | solution.py:171
  118.5 0.7 copy-done.8
  119.5 0.2 multiply_reduce_fusion
  119.7 3.3 %all-to-all-start.2 = ((f32[8,1,192]{2,1,0:T(1,128)}), f32[8,1,192]{2,1,0:T(1,128)S(1)}, u32[]{:S(2)}, u32[]{:S(2)}) async-start(f32[8,1,192]{2,1,0:T(1,128)} %get-tuple-element.19), calls=%async_computation.3 | async-start | bytes 16384 | tf_op jit(solution)/shard_map/all_to_all | solution.py:212
  123.1 0.6 fusion.14
  123.8 1.3 multiply_reduce_fusion.1
  127.7 1.9 all-to-all-done.2
  129.8 0.6 convert.2
  130.4 13.5 %all-to-all-start.3 = ((bf16[64,1,3]{2,1,0:T(2,128)(2,1)}), bf16[64,1,3]{2,1,0:T(2,128)(2,1)S(1)}, u32[]{:S(2)}, u32[]{:S(2)}) async-start(bf16[64,1,3]{2,1,0:T(2,128)(2,1)} %convert.2), calls=%async_computation.4 | async-start | bytes 65536 | tf_op jit(solution)/shard_map/all_to_all | solution.py:214
  144.0 9.3 %all-to-all-done.3 = bf16[64,1,3]{2,1,0:T(2,128)(2,1)S(1)} async-done(((bf16[64,1,3]{2,1,0:T(2,128)(2,1)}), bf16[64,1,3]{2,1,0:T(2,128)(2,1)S(1)}, u32[]{:S(2)}, u32[]{:S(2)}) %all-to-all-start.3) | async-done | bytes 416 | tf_op jit(solution)/shard_map/all_to_all | solution.py:214
  153.7 0.4 convolution_bitcast_fusion
  154.0 0.3 copy.97
  154.4 0.7 reshape.118
  155.0 21.8 %all_to_all.36 = f32[64,1,2048]{2,1,0:T(1,128)S(1)} all-to-all(f32[64,1,2048]{2,1,0:T(1,128)S(1)} %reshape.118), channel_id=1, replica_groups=mesh['expert'=64,'dp'=8] {'expert'}, dimensions={0} | all-to-all | bytes 1048576 | tf_op jit(solution)/shard_map/all_to_all | solution.py:231
  176.8 0.5 broadcast.119
  177.3 1.9 reduce.3
  179.2 0.4 reshape.119
  179.8 10.5 %all_to_all.37 = f32[8,1,256]{2,1,0:T(1,128)S(1)} all-to-all(f32[8,1,256]{2,1,0:T(1,128)S(1)} %reshape.120), channel_id=1, replica_groups=mesh['expert'=64,'dp'=8] {'dp'}, dimensions={0} | all-to-all | bytes 16384 | tf_op jit(solution)/shard_map/all_to_all | solution.py:233
  190.3 0.7 reduce.4
  191.1 0.6 reduce_sum.79
  191.7 3.5 %reduce-scatter.2.cloned.1.call-done = bf16[192,2048]{1,0:T(8,128)(2,1)} async-done(((bf16[1536,2048]{1,0:T(8,128)(2,1)}), bf16[192,2048]{1,0:T(8,128)(2,1)}) %reduce-scatter.2.cloned.1.call-update) | async-done | bytes 786448 | tf_op jit(solution)/shard_map/reduce_scatter | solution.py:197
  195.2 1.4 reshape.109
  196.7 32.9 %all_to_all.38 = bf16[64,48,128]{2,1,0:T(8,128)(2,1)S(1)} all-to-all(bf16[64,48,128]{2,1,0:T(8,128)(2,1)S(1)} %reshape.109), channel_id=1, replica_groups=mesh['expert'=64,'dp'=8] {'expert'}, dimensions={0} | all-to-all | bytes 1572864 | tf_op jit(solution)/shard_map/all_to_all | solution.py:237
  229.5 0.3 reshape.110
  229.9 0.4 convolution_multiply_fusion
  230.2 0.3 copy-done.7
  230.5 1.2 fusion.1
  (38 shorter events, 1.5 us)
Async XLA Ops:
  7.2 10.0 %copy-start = (bf16[128,2048]{1,0:T(8,128)(2,1)S(1)}, bf16[128,2048]{1,0:T(8,128)(2,1)}, u32[]{:S(2)}) copy-start(bf16[128,2048]{1,0:T(8,128)(2,1)} %param.13) | copy-start | bytes 1572868
  7.2 81.4 %all-gather.3.cloned.1.call-start = ((), (), s32[]{:S(2)}) async-start(), calls=%async_computation.9 | async-start | bytes 6488064 | tf_op jit(solution)/shard_map/all_gather | solution.py:101
  18.9 12.0 %copy-start.5 = (bf16[1,64,8,3,2,176]{5,4,3,2,1,0:T(2,128)(2,1)S(1)}, bf16[1,64,8,3,2,176]{5,4,3,2,1,0:T(2,128)(2,1)}, u32[]{:S(2)}) copy-start(bf16[1,64,8,3,2,176]{5,4,3,2,1,0:T(2,128)(2,1)} %param.20) | copy-start | bytes 3244036
  18.9 39.9 %all-to-all-start = ((bf16[64,4,2048]{2,1,0:T(4,128)(2,1)}), bf16[64,4,2048]{2,1,0:T(4,128)(2,1)}, u32[]{:S(2)}, u32[]{:S(2)}) async-start(bf16[64,4,2048]{2,1,0:T(4,128)(2,1)} %reshape.103), calls=%async_computation | async-start | bytes 2097152 | tf_op jit(solution)/shard_map/all_to_all | solution.py:129
  30.8 164.4 %reduce-scatter.2.cloned.1.call-start = ((), (), s32[]{:S(2)}) async-start(), calls=%async_computation.8 | async-start | bytes 7077888 | tf_op jit(solution)/shard_map/reduce_scatter | solution.py:197
  88.6 24.1 %copy-start.1 = (f32[8,176,192]{2,1,0:T(8,128)S(1)}, f32[8,176,192]{2,1,0:T(8,128)}, u32[]{:S(2)}) copy-start(f32[8,176,192]{2,1,0:T(8,128)} %get-tuple-element.15.scale_a_ref) | copy-start | bytes 3244036
  88.6 24.1 %copy-start.2 = (f32[8,176,192]{2,1,0:T(8,128)S(1)}, f32[8,176,192]{2,1,0:T(8,128)}, u32[]{:S(2)}) copy-start(f32[8,176,192]{2,1,0:T(8,128)} %get-tuple-element.16.scale_b_ref) | copy-start | bytes 3244036
  88.6 24.1 %copy-start.3 = (bf16[1,2048,176]{1,2,0:T(8,128)(2,1)S(1)}, bf16[1,2048,176]{1,2,0:T(8,128)(2,1)}, u32[]{:S(2)}) copy-start(bf16[1,2048,176]{1,2,0:T(8,128)(2,1)} %param.17) | copy-start | bytes 2162692
  88.6 24.1 %copy-start.4 = (bf16[1,2048,176]{1,2,0:T(8,128)(2,1)S(1)}, bf16[1,2048,176]{1,2,0:T(8,128)(2,1)}, u32[]{:S(2)}) copy-start(bf16[1,2048,176]{1,2,0:T(8,128)(2,1)} %param.18) | copy-start | bytes 2162692
  118.5 0.8 copy-start.8
  118.5 1.1 copy-start.9
  118.5 35.2 %copy-start.6 = (bf16[128,2048]{1,0:T(8,128)(2,1)S(1)}, bf16[128,2048]{1,0:T(8,128)(2,1)}, u32[]{:S(2)}) copy-start(bf16[128,2048]{1,0:T(8,128)(2,1)} %param.12) | copy-start | bytes 1572868
  119.7 9.9 %all-to-all-start.2 = ((f32[8,1,192]{2,1,0:T(1,128)}), f32[8,1,192]{2,1,0:T(1,128)S(1)}, u32[]{:S(2)}, u32[]{:S(2)}) async-start(f32[8,1,192]{2,1,0:T(1,128)} %get-tuple-element.19), calls=%async_computation.3 | async-start | bytes 16384 | tf_op jit(solution)/shard_map/all_to_all | solution.py:212
  130.4 22.8 %all-to-all-start.3 = ((bf16[64,1,3]{2,1,0:T(2,128)(2,1)}), bf16[64,1,3]{2,1,0:T(2,128)(2,1)S(1)}, u32[]{:S(2)}, u32[]{:S(2)}) async-start(bf16[64,1,3]{2,1,0:T(2,128)(2,1)} %convert.2), calls=%async_computation.4 | async-start | bytes 65536 | tf_op jit(solution)/shard_map/all_to_all | solution.py:214
  229.5 1.0 copy-start.7
Sparse Core Ops, SparseCore 0:
  10.1 78.4 all-gather.2
  118.6 76.5 reduce-scatter.1

commit v4 on v3

--- a/solution.py
+++ b/solution.py
@@ -233,7 +233,10 @@
     router_part = lax.all_to_all(router_part, "dp", split_axis=0, concat_axis=0, tiled=True)
     router_grad = jnp.sum(router_part, axis=0).T
 
-    routed, router_grad = lax.optimization_barrier((routed, router_grad))
+    router_term = jnp.dot(logit_grad, router_weight, preferred_element_type=f32)
+    routed, router_grad, router_term, chosen_prob, placer = lax.optimization_barrier(
+        (routed, router_grad, router_term, chosen_prob, placer)
+    )
     homeward = lax.all_to_all(
         routed.reshape(expert_count, rows * width // expert_count // LANES, LANES),
         "expert",
@@ -244,10 +247,7 @@
     routed_tok = jnp.einsum(
         "st,sd->td", placer, homeward.reshape(rows, width), preferred_element_type=f32
     )
-    input_grad = (
-        chosen_prob[:, None] * routed_tok
-        + jnp.dot(logit_grad, router_weight, preferred_element_type=f32)
-    ).astype(bf16)
+    input_grad = (chosen_prob[:, None] * routed_tok + router_term).astype(bf16)
     return (input_grad, router_grad)
 
 

time: 239 us -> 239 us (level)
  blocking collectives: 85.3 us -> 53 us
  waiting for transfers between devices: 56.6 us -> 78.8 us
  starting transfers between devices: 28.9 us -> 37.3 us
    all_to_all x2 -> x0, blocking collectives: 32.3 us -> none  [the longest x1 21.8 us: local(): lax.all_to_all(router_part, 'expert', split_axis=0, concat_axis=0, tiled=...]
    all_to_all x0 -> x2, waiting for transfers between devices: none -> 24.4 us  [the longest x1 17.8 us: local(): lax.all_to_all(router_part, 'expert', split_axis=0, concat_axis=0, tiled=...]
    all_to_all x0 -> x2, starting transfers between devices: none -> 8.38 us  [the longest x1 4.74 us: local(): lax.all_to_all(router_part, 'expert', split_axis=0, concat_axis=0, tiled=...]
  transfers between devices with their start and end apart: 5 -> 7, of which waited for: 5 -> 7; matrix products, arithmetic and copies ran while one was open for 13% -> 14% of each run, Pallas kernels for 0% -> 0%
where the time goes in v4:
time: 239 us; the launch traced here: 238 us
  waiting for transfers between devices  78.8 us (33%)
  blocking collectives  53 us (22%)
  starting transfers between devices  37.3 us (16%)
  between operations  21.7 us (9%)
  local copies, waits for them, and re-layouts  18.6 us (8%)
  other arithmetic  16.3 us (7%)
  Pallas kernels  9.67 us (4%)
  matrix products  2.44 us (1%)
    all_to_all x1, blocking collectives, local(): lax.all_to_all(routed.reshape(expert_count, rows * width // expert_count...  32.9 us
    all_gather x1, waiting for transfers between devices, local(): down_full = lax.all_gather(down_weight[0], 'dp', axis=0, tiled=True)  26.6 us
    all_to_all x1, blocking collectives, local(): lax.all_to_all(packed, 'dp', split_axis=0, concat_axis=0, tiled=True)  20.1 us
    all_to_all x1, waiting for transfers between devices, local(): lax.all_to_all(router_part, 'expert', split_axis=0, concat_axis=0, tiled=...  17.8 us
    all_to_all x1, waiting for transfers between devices, local(): lax.all_to_all(outgoing, 'expert', split_axis=0, concat_axis=0, tiled=True)  14.6 us
    all_to_all x1, starting transfers between devices, local(): lax.all_to_all(gate_sum, 'expert', split_axis=0, concat_axis=0, tiled=True)  13.5 us
    all_to_all x1, starting transfers between devices, local(): lax.all_to_all(outgoing, 'expert', split_axis=0, concat_axis=0, tiled=True)  11.9 us
    all_to_all x1, waiting for transfers between devices, local(): lax.all_to_all(gate_sum, 'expert', split_axis=0, concat_axis=0, tiled=True)  9.29 us
  transfers between devices with their start and end apart: 7, of which 7 were waited for; matrix products, arithmetic and copies ran while one was open for 14% of the time, Pallas kernels for 0%

profile of v4, /device:TPU:1, one launch (start us, length us, event | category | flops | bytes accessed | tf_op | source)
XLA Modules:
  0.0 237.8 jit_solution(17012614337054264193)
XLA Ops:
  7.2 0.7 all-gather.3.cloned.1.call-update
  12.8 0.7 fusion.7
  13.8 1.9 select_select_fusion
  15.7 0.8 select_reduce_fusion
  16.5 0.7 multiply_add_fusion
  17.2 0.4 fusion
  17.6 1.2 reshape.101
  18.9 11.9 %all-to-all-start = ((bf16[64,4,2048]{2,1,0:T(4,128)(2,1)}), bf16[64,4,2048]{2,1,0:T(4,128)(2,1)}, u32[]{:S(2)}, u32[]{:S(2)}) async-start(bf16[64,4,2048]{2,1,0:T(4,128)(2,1)} %reshape.101), calls=%async_computation | async-start | bytes 2097152 | tf_op jit(solution)/shard_map/all_to_all | solution.py:129
  30.9 0.5 copy.107
  31.4 1.5 slice_convert_fusion.1
  32.9 0.9 copy.85
  33.8 1.9 copy.86
  35.7 2.3 copy.84
  38.0 1.9 copy.87
  39.9 4.2 %fusion.15 = (f32[8,176,192]{2,1,0:T(8,128)S(1)}, f32[8,176,192]{2,1,0:T(8,128)}, f32[8,176,192]{2,1,0:T(8,128)}) fusion(f32[8,176,192]{2,1,0:T(8,128)} %copy.87, f32[8,176,192]{2,1,0:T(8,128)} %copy.86), kind=kLoop, calls=%fused_computation.51 | loop fusion | flops 2703360 | bytes 5406720 | tf_op jit(solution)/shard_map/mul | solution.py:138
  44.2 14.6 %all-to-all-done = bf16[64,4,2048]{2,1,0:T(4,128)(2,1)} async-done(((bf16[64,4,2048]{2,1,0:T(4,128)(2,1)}), bf16[64,4,2048]{2,1,0:T(4,128)(2,1)}, u32[]{:S(2)}, u32[]{:S(2)}) %all-to-all-start) | async-done | bytes 1048608 | tf_op jit(solution)/shard_map/all_to_all | solution.py:129
  58.7 2.4 %reshape.102.refs_4_ = bf16[192,2048]{1,0:T(8,128)(2,1)S(1)} reshape(bf16[64,3,2048]{2,1,0:T(4,128)(2,1)} %bitcast.56) | data formatting | bytes 1572864 | tf_op jit(solution)/shard_map/reshape | solution.py:130
  61.1 0.9 slice.47
  62.0 26.6 %all-gather.3.cloned.1.call-done = bf16[1,1408,2048]{2,1,0:T(8,128)(2,1)} async-done(((bf16[1,176,2048]{2,1,0:T(8,128)(2,1)}), bf16[1,1408,2048]{2,1,0:T(8,128)(2,1)}) %all-gather.3.cloned.1.call-update) | async-done | bytes 5767184 | tf_op jit(solution)/shard_map/all_gather | solution.py:101
  88.6 4.0 %shard_map.131 = bf16[8,272,128]{2,1,0:T(8,128)(2,1)S(1)} custom-call(bf16[1408,2048]{1,0:T(8,128)(2,1)} %bitcast.68, bf16[1408,2048]{1,0:T(8,128)(2,1)} %bitcast.69, bf16[1408,2048]{1,0:T(8,128)(2,1)} %bitcast.70, bf16[1408,2048]{1,0:T(8,128)(2,1)} %bitcast.71, bf16[192,2048]{1,0:T(8,128)(2,1)S(1)} %reshape.102.refs_4_, bf16[64,128]{1,0:T(8,128)(2,1)S(1)} %bitcast.65), custom_call_target="tpu_custom_call" | custom-call | flops 1107296256 | bytes 5767168 | tf_op jit(solution)/shard_map/pallas_call | solution.py:145
  92.6 20.1 %all_to_all.35.packed_ref = bf16[8,272,128]{2,1,0:T(8,128)(2,1)S(1)} all-to-all(bf16[8,272,128]{2,1,0:T(8,128)(2,1)S(1)} %shard_map.131), channel_id=1, replica_groups=mesh['expert'=64,'dp'=8] {'dp'}, dimensions={0} | all-to-all | bytes 1114112 | tf_op jit(solution)/shard_map/all_to_all | solution.py:169
  112.8 5.7 %shard_map.132 = (bf16[8,192,2048]{2,1,0:T(8,128)(2,1)}, f32[8,1,192]{2,1,0:T(1,128)}) custom-call(bf16[8,272,128]{2,1,0:T(8,128)(2,1)S(1)} %all_to_all.35.packed_ref, f32[8,176,192]{2,1,0:T(8,128)S(1)} %copy-done.1, f32[8,176,192]{2,1,0:T(8,128)S(1)} %copy-done.2, f32[8,176,192]{2,1,0:T(8,128)S(1)} %get-tuple-element.20.scale_g_ref, ...), custom_call_target="tpu_custom_call" | custom-call | flops 2214592512 | bytes 6291456 | tf_op jit(solution)/shard_map/pallas_call | solution.py:171
  118.5 0.7 copy-done.8
  119.7 3.3 %all-to-all-start.2 = ((f32[8,1,192]{2,1,0:T(1,128)}), f32[8,1,192]{2,1,0:T(1,128)S(1)}, u32[]{:S(2)}, u32[]{:S(2)}) async-start(f32[8,1,192]{2,1,0:T(1,128)} %get-tuple-element.22), calls=%async_computation.3 | async-start | bytes 16384 | tf_op jit(solution)/shard_map/all_to_all | solution.py:212
  123.1 0.6 fusion.16
  123.8 1.3 multiply_reduce_fusion.1
  127.6 2.1 all-to-all-done.2
  129.8 0.6 convert.2
  130.4 13.5 %all-to-all-start.3 = ((bf16[64,1,3]{2,1,0:T(2,128)(2,1)}), bf16[64,1,3]{2,1,0:T(2,128)(2,1)S(1)}, u32[]{:S(2)}, u32[]{:S(2)}) async-start(bf16[64,1,3]{2,1,0:T(2,128)(2,1)} %convert.2), calls=%async_computation.4 | async-start | bytes 65536 | tf_op jit(solution)/shard_map/all_to_all | solution.py:214
  144.0 9.3 %all-to-all-done.3 = bf16[64,1,3]{2,1,0:T(2,128)(2,1)S(1)} async-done(((bf16[64,1,3]{2,1,0:T(2,128)(2,1)}), bf16[64,1,3]{2,1,0:T(2,128)(2,1)S(1)}, u32[]{:S(2)}, u32[]{:S(2)}) %all-to-all-start.3) | async-done | bytes 416 | tf_op jit(solution)/shard_map/all_to_all | solution.py:214
  153.7 0.4 convolution_bitcast_fusion
  154.4 1.5 reshape.116
  155.8 4.7 %all-to-all-start.4 = ((f32[64,1,2048]{2,1,0:T(1,128)}), f32[64,1,2048]{2,1,0:T(1,128)S(1)}, u32[]{:S(2)}, u32[]{:S(2)}) async-start(f32[64,1,2048]{2,1,0:T(1,128)} %reshape.116), calls=%async_computation.5 | async-start | bytes 1048576 | tf_op jit(solution)/shard_map/all_to_all | solution.py:231
  160.6 17.8 %all-to-all-done.4 = f32[64,1,2048]{2,1,0:T(1,128)S(1)} async-done(((f32[64,1,2048]{2,1,0:T(1,128)}), f32[64,1,2048]{2,1,0:T(1,128)S(1)}, u32[]{:S(2)}, u32[]{:S(2)}) %all-to-all-start.4) | async-done | bytes 524320 | tf_op jit(solution)/shard_map/all_to_all | solution.py:231
  178.4 0.5 broadcast.116
  178.9 1.9 reduce.3
  180.8 0.4 reshape.117
  181.4 0.7 reshape.118
  182.0 3.6 %all-to-all-start.5 = ((f32[8,1,256]{2,1,0:T(1,128)}), f32[8,1,256]{2,1,0:T(1,128)S(1)}, u32[]{:S(2)}, u32[]{:S(2)}) async-start(f32[8,1,256]{2,1,0:T(1,128)} %reshape.118), calls=%async_computation.6 | async-start | bytes 16384 | tf_op jit(solution)/shard_map/all_to_all | solution.py:233
  185.7 0.4 fusion.14
  186.1 6.6 %all-to-all-done.5 = f32[8,1,256]{2,1,0:T(1,128)S(1)} async-done(((f32[8,1,256]{2,1,0:T(1,128)}), f32[8,1,256]{2,1,0:T(1,128)S(1)}, u32[]{:S(2)}, u32[]{:S(2)}) %all-to-all-start.5) | async-done | bytes 8224 | tf_op jit(solution)/shard_map/all_to_all | solution.py:233
  192.6 0.7 reduce.4
  193.4 0.6 reduce_sum.79
  194.0 1.2 reduce-scatter.2.cloned.1.call-done
  195.2 1.4 reshape.107
  196.6 32.9 %all_to_all.36 = bf16[64,48,128]{2,1,0:T(8,128)(2,1)S(1)} all-to-all(bf16[64,48,128]{2,1,0:T(8,128)(2,1)S(1)} %reshape.107), channel_id=1, replica_groups=mesh['expert'=64,'dp'=8] {'expert'}, dimensions={0} | all-to-all | bytes 1572864 | tf_op jit(solution)/shard_map/all_to_all | solution.py:240
  229.5 0.3 reshape.108
  229.9 1.1 fusion.2
  (41 shorter events, 1.9 us)
Async XLA Ops:
  7.2 10.0 %copy-start = (bf16[128,2048]{1,0:T(8,128)(2,1)S(1)}, bf16[128,2048]{1,0:T(8,128)(2,1)}, u32[]{:S(2)}) copy-start(bf16[128,2048]{1,0:T(8,128)(2,1)} %param.13) | copy-start | bytes 1572868
  7.2 81.4 %all-gather.3.cloned.1.call-start = ((), (), s32[]{:S(2)}) async-start(), calls=%async_computation.9 | async-start | bytes 6488064 | tf_op jit(solution)/shard_map/all_gather | solution.py:101
  18.9 12.0 %copy-start.5 = (bf16[1,64,8,3,2,176]{5,4,3,2,1,0:T(2,128)(2,1)S(1)}, bf16[1,64,8,3,2,176]{5,4,3,2,1,0:T(2,128)(2,1)}, u32[]{:S(2)}) copy-start(bf16[1,64,8,3,2,176]{5,4,3,2,1,0:T(2,128)(2,1)} %param.20) | copy-start | bytes 3244036
  18.9 39.9 %all-to-all-start = ((bf16[64,4,2048]{2,1,0:T(4,128)(2,1)}), bf16[64,4,2048]{2,1,0:T(4,128)(2,1)}, u32[]{:S(2)}, u32[]{:S(2)}) async-start(bf16[64,4,2048]{2,1,0:T(4,128)(2,1)} %reshape.101), calls=%async_computation | async-start | bytes 2097152 | tf_op jit(solution)/shard_map/all_to_all | solution.py:129
  30.8 164.4 %reduce-scatter.2.cloned.1.call-start = ((), (), s32[]{:S(2)}) async-start(), calls=%async_computation.8 | async-start | bytes 7077888 | tf_op jit(solution)/shard_map/reduce_scatter | solution.py:197
  88.6 24.1 %copy-start.1 = (f32[8,176,192]{2,1,0:T(8,128)S(1)}, f32[8,176,192]{2,1,0:T(8,128)}, u32[]{:S(2)}) copy-start(f32[8,176,192]{2,1,0:T(8,128)} %get-tuple-element.18.scale_a_ref) | copy-start | bytes 3244036
  88.6 24.1 %copy-start.2 = (f32[8,176,192]{2,1,0:T(8,128)S(1)}, f32[8,176,192]{2,1,0:T(8,128)}, u32[]{:S(2)}) copy-start(f32[8,176,192]{2,1,0:T(8,128)} %get-tuple-element.19.scale_b_ref) | copy-start | bytes 3244036
  88.6 24.1 %copy-start.3 = (bf16[1,2048,176]{1,2,0:T(8,128)(2,1)S(1)}, bf16[1,2048,176]{1,2,0:T(8,128)(2,1)}, u32[]{:S(2)}) copy-start(bf16[1,2048,176]{1,2,0:T(8,128)(2,1)} %param.17) | copy-start | bytes 2162692
  88.6 24.1 %copy-start.4 = (bf16[1,2048,176]{1,2,0:T(8,128)(2,1)S(1)}, bf16[1,2048,176]{1,2,0:T(8,128)(2,1)}, u32[]{:S(2)}) copy-start(bf16[1,2048,176]{1,2,0:T(8,128)(2,1)} %param.18) | copy-start | bytes 2162692
  118.5 0.8 copy-start.8
  118.5 1.1 copy-start.9
  118.5 35.2 %copy-start.6 = (bf16[128,2048]{1,0:T(8,128)(2,1)S(1)}, bf16[128,2048]{1,0:T(8,128)(2,1)}, u32[]{:S(2)}) copy-start(bf16[128,2048]{1,0:T(8,128)(2,1)} %param.12) | copy-start | bytes 1572868
  119.7 9.9 %all-to-all-start.2 = ((f32[8,1,192]{2,1,0:T(1,128)}), f32[8,1,192]{2,1,0:T(1,128)S(1)}, u32[]{:S(2)}, u32[]{:S(2)}) async-start(f32[8,1,192]{2,1,0:T(1,128)} %get-tuple-element.22), calls=%async_computation.3 | async-start | bytes 16384 | tf_op jit(solution)/shard_map/all_to_all | solution.py:212
  130.4 22.8 %all-to-all-start.3 = ((bf16[64,1,3]{2,1,0:T(2,128)(2,1)}), bf16[64,1,3]{2,1,0:T(2,128)(2,1)S(1)}, u32[]{:S(2)}, u32[]{:S(2)}) async-start(bf16[64,1,3]{2,1,0:T(2,128)(2,1)} %convert.2), calls=%async_computation.4 | async-start | bytes 65536 | tf_op jit(solution)/shard_map/all_to_all | solution.py:214
  155.8 22.6 %all-to-all-start.4 = ((f32[64,1,2048]{2,1,0:T(1,128)}), f32[64,1,2048]{2,1,0:T(1,128)S(1)}, u32[]{:S(2)}, u32[]{:S(2)}) async-start(f32[64,1,2048]{2,1,0:T(1,128)} %reshape.116), calls=%async_computation.5 | async-start | bytes 1048576 | tf_op jit(solution)/shard_map/all_to_all | solution.py:231
  180.8 4.9 %copy-start.7 = (bf16[64,2048]{1,0:T(8,128)(2,1)S(1)}, bf16[64,2048]{1,0:T(8,128)(2,1)}, u32[]{:S(2)}) copy-start(bf16[64,2048]{1,0:T(8,128)(2,1)} %param.16) | copy-start | bytes 786436
  182.0 10.6 %all-to-all-start.5 = ((f32[8,1,256]{2,1,0:T(1,128)}), f32[8,1,256]{2,1,0:T(1,128)S(1)}, u32[]{:S(2)}, u32[]{:S(2)}) async-start(f32[8,1,256]{2,1,0:T(1,128)} %reshape.118), calls=%async_computation.6 | async-start | bytes 16384 | tf_op jit(solution)/shard_map/all_to_all | solution.py:233
Sparse Core Ops, SparseCore 0:
  10.1 78.4 all-gather.2
  118.6 76.5 reduce-scatter.1

commit v5 on v4

--- a/solution.py
+++ b/solution.py
@@ -12,8 +12,7 @@
 RECORD_ROWS = 8
 DOWN_PIECES = 4
 DOWN_HOLDERS = 4
-UP_SENDERS = 2
-UP_CHUNKS = 4
+UP_CHUNKS = 2
 VMEM_GRANT = 32 * 2**20
 
 
@@ -47,7 +46,16 @@
 
 
 def up_kernel(
-    packed_ref, scale_a_ref, scale_b_ref, scale_g_ref, gate_ref, up_ref, part_ref, gate_part_ref
+    packed_ref,
+    scale_a_ref,
+    scale_b_ref,
+    scale_g_ref,
+    gate_ref,
+    up_ref,
+    part_ref,
+    gate_part_ref,
+    held,
+    sems,
 ):
     senders = packed_ref.shape[0]
     hidden, width = gate_ref.shape
@@ -55,6 +63,7 @@
     seam = LANES // 2
     span = width // UP_CHUNKS
     f32, bf16 = jnp.float32, jnp.bfloat16
+    copies = []
     for sender in range(senders):
         head = packed_ref[sender, :hidden, :].astype(f32)
         tail = packed_ref[sender, hidden:, :].astype(f32)[:half]
@@ -67,7 +76,16 @@
             columns = slice(chunk * span, (chunk + 1) * span)
             part = jnp.dot(grad_a, gate_ref[:, columns], preferred_element_type=f32)
             part = part + jnp.dot(grad_b, up_ref[:, columns], preferred_element_type=f32)
-            part_ref[sender, :, columns] = part.astype(bf16)
+            held[sender, :, columns] = part.astype(bf16)
+            copy = pltpu.make_async_copy(
+                held.at[sender, :, pl.ds(chunk * span, span)],
+                part_ref.at[sender, :, pl.ds(chunk * span, span)],
+                sems.at[sender, chunk],
+            )
+            copy.start()
+            copies.append(copy)
+    for copy in copies:
+        copy.wait()
 
 
 def piece_index(place, i):
@@ -170,18 +188,14 @@
 
     part, gate_parts = pl.pallas_call(
         up_kernel,
-        grid=(dp_count // UP_SENDERS,),
-        in_specs=[
-            pl.BlockSpec((UP_SENDERS, packed_rows, LANES), lambda i: (i, 0, 0)),
-            pl.BlockSpec((UP_SENDERS, hidden, rows), lambda i: (i, 0, 0)),
-            pl.BlockSpec((UP_SENDERS, hidden, rows), lambda i: (i, 0, 0)),
-            pl.BlockSpec((UP_SENDERS, hidden, rows), lambda i: (i, 0, 0)),
-            pl.BlockSpec((hidden, width), lambda i: (0, 0)),
-            pl.BlockSpec((hidden, width), lambda i: (0, 0)),
-        ],
+        in_specs=[pl.BlockSpec(memory_space=pltpu.VMEM)] * 6,
         out_specs=[
-            pl.BlockSpec((UP_SENDERS, rows, width), lambda i: (i, 0, 0)),
-            pl.BlockSpec((UP_SENDERS, 1, rows), lambda i: (i, 0, 0)),
+            pl.BlockSpec(memory_space=pl.ANY),
+            pl.BlockSpec(memory_space=pltpu.VMEM),
+        ],
+        scratch_shapes=[
+            pltpu.VMEM((dp_count, rows, width), bf16),
+            pltpu.SemaphoreType.DMA((dp_count, UP_CHUNKS)),
         ],
         out_shape=[
             pltpu.HBM((dp_count, rows, width), bf16),

time: 239 us -> 238 us (level)
  no operation moved by 1% of the time
where the time goes in v5:
time: 238 us; the launch traced here: 237 us
  waiting for transfers between devices  78.8 us (33%)
  blocking collectives  53 us (22%)
  starting transfers between devices  37.3 us (16%)
  between operations  21.8 us (9%)
  local copies, waits for them, and re-layouts  18.6 us (8%)
  other arithmetic  16.3 us (7%)
  Pallas kernels  9.08 us (4%)
  matrix products  2.42 us (1%)
    all_to_all x1, blocking collectives, local(): lax.all_to_all(routed.reshape(expert_count, rows * width // expert_count...  32.9 us
    all_gather x1, waiting for transfers between devices, local(): down_full = lax.all_gather(down_weight[0], 'dp', axis=0, tiled=True)  26.6 us
    all_to_all x1, blocking collectives, local(): lax.all_to_all(packed, 'dp', split_axis=0, concat_axis=0, tiled=True)  20.1 us
    all_to_all x1, waiting for transfers between devices, local(): lax.all_to_all(router_part, 'expert', split_axis=0, concat_axis=0, tiled=...  17.8 us
    all_to_all x1, waiting for transfers between devices, local(): lax.all_to_all(outgoing, 'expert', split_axis=0, concat_axis=0, tiled=True)  14.6 us
    all_to_all x1, starting transfers between devices, local(): lax.all_to_all(gate_sum, 'expert', split_axis=0, concat_axis=0, tiled=True)  13.5 us
    all_to_all x1, starting transfers between devices, local(): lax.all_to_all(outgoing, 'expert', split_axis=0, concat_axis=0, tiled=True)  11.9 us
    all_to_all x1, waiting for transfers between devices, local(): lax.all_to_all(gate_sum, 'expert', split_axis=0, concat_axis=0, tiled=True)  9.29 us
  transfers between devices with their start and end apart: 7, of which 7 were waited for; matrix products, arithmetic and copies ran while one was open for 14% of the time, Pallas kernels for 0%

profile of v5, /device:TPU:1, one launch (start us, length us, event | category | flops | bytes accessed | tf_op | source)
XLA Modules:
  0.0 237.3 jit_solution(17467108033344354230)
XLA Ops:
  7.2 0.7 all-gather.3.cloned.1.call-update
  12.8 0.7 fusion.7
  13.8 1.9 select_select_fusion
  15.7 0.8 select_reduce_fusion
  16.5 0.7 multiply_add_fusion
  17.2 0.4 fusion
  17.6 1.2 reshape.101
  18.9 11.9 %all-to-all-start = ((bf16[64,4,2048]{2,1,0:T(4,128)(2,1)}), bf16[64,4,2048]{2,1,0:T(4,128)(2,1)}, u32[]{:S(2)}, u32[]{:S(2)}) async-start(bf16[64,4,2048]{2,1,0:T(4,128)(2,1)} %reshape.101), calls=%async_computation | async-start | bytes 2097152 | tf_op jit(solution)/shard_map/all_to_all | solution.py:147
  30.9 0.5 copy.107
  31.4 1.5 slice_convert_fusion.1
  32.9 0.9 copy.85
  33.8 1.9 copy.86
  35.7 2.3 copy.84
  38.0 1.9 copy.87
  39.9 4.2 %fusion.15 = (f32[8,176,192]{2,1,0:T(8,128)S(1)}, f32[8,176,192]{2,1,0:T(8,128)}, f32[8,176,192]{2,1,0:T(8,128)}) fusion(f32[8,176,192]{2,1,0:T(8,128)} %copy.87, f32[8,176,192]{2,1,0:T(8,128)} %copy.86), kind=kLoop, calls=%fused_computation.51 | loop fusion | flops 2703360 | bytes 5406720 | tf_op jit(solution)/shard_map/mul | solution.py:156
  44.2 14.6 %all-to-all-done = bf16[64,4,2048]{2,1,0:T(4,128)(2,1)} async-done(((bf16[64,4,2048]{2,1,0:T(4,128)(2,1)}), bf16[64,4,2048]{2,1,0:T(4,128)(2,1)}, u32[]{:S(2)}, u32[]{:S(2)}) %all-to-all-start) | async-done | bytes 1048608 | tf_op jit(solution)/shard_map/all_to_all | solution.py:147
  58.7 2.4 %reshape.102.refs_4_ = bf16[192,2048]{1,0:T(8,128)(2,1)S(1)} reshape(bf16[64,3,2048]{2,1,0:T(4,128)(2,1)} %bitcast.56) | data formatting | bytes 1572864 | tf_op jit(solution)/shard_map/reshape | solution.py:148
  61.1 0.9 slice.47
  62.0 26.6 %all-gather.3.cloned.1.call-done = bf16[1,1408,2048]{2,1,0:T(8,128)(2,1)} async-done(((bf16[1,176,2048]{2,1,0:T(8,128)(2,1)}), bf16[1,1408,2048]{2,1,0:T(8,128)(2,1)}) %all-gather.3.cloned.1.call-update) | async-done | bytes 5767184 | tf_op jit(solution)/shard_map/all_gather | solution.py:119
  88.6 4.0 %shard_map.131 = bf16[8,272,128]{2,1,0:T(8,128)(2,1)S(1)} custom-call(bf16[1408,2048]{1,0:T(8,128)(2,1)} %bitcast.68, bf16[1408,2048]{1,0:T(8,128)(2,1)} %bitcast.69, bf16[1408,2048]{1,0:T(8,128)(2,1)} %bitcast.70, bf16[1408,2048]{1,0:T(8,128)(2,1)} %bitcast.71, bf16[192,2048]{1,0:T(8,128)(2,1)S(1)} %reshape.102.refs_4_, bf16[64,128]{1,0:T(8,128)(2,1)S(1)} %bitcast.65), custom_call_target="tpu_custom_call" | custom-call | flops 1107296256 | bytes 5767168 | tf_op jit(solution)/shard_map/pallas_call | solution.py:163
  92.6 20.1 %all_to_all.35.packed_ref = bf16[8,272,128]{2,1,0:T(8,128)(2,1)S(1)} all-to-all(bf16[8,272,128]{2,1,0:T(8,128)(2,1)S(1)} %shard_map.131), channel_id=1, replica_groups=mesh['expert'=64,'dp'=8] {'dp'}, dimensions={0} | all-to-all | bytes 1114112 | tf_op jit(solution)/shard_map/all_to_all | solution.py:187
  112.8 5.1 %shard_map.132 = (bf16[8,192,2048]{2,1,0:T(8,128)(2,1)}, f32[8,1,192]{2,1,0:T(1,128)}) custom-call(bf16[8,272,128]{2,1,0:T(8,128)(2,1)S(1)} %all_to_all.35.packed_ref, f32[8,176,192]{2,1,0:T(8,128)S(1)} %copy-done.1, f32[8,176,192]{2,1,0:T(8,128)S(1)} %copy-done.2, f32[8,176,192]{2,1,0:T(8,128)S(1)} %get-tuple-element.20.scale_g_ref, ...), custom_call_target="tpu_custom_call" | custom-call | flops 2214592512 | bytes 6291456 | tf_op jit(solution)/shard_map/pallas_call | solution.py:189
  117.9 0.7 copy-done.8
  119.2 3.3 %all-to-all-start.2 = ((f32[8,1,192]{2,1,0:T(1,128)}), f32[8,1,192]{2,1,0:T(1,128)S(1)}, u32[]{:S(2)}, u32[]{:S(2)}) async-start(f32[8,1,192]{2,1,0:T(1,128)} %get-tuple-element.22), calls=%async_computation.3 | async-start | bytes 16384 | tf_op jit(solution)/shard_map/all_to_all | solution.py:226
  122.6 0.6 fusion.16
  123.2 1.3 multiply_reduce_fusion.1
  127.0 2.1 all-to-all-done.2
  129.2 0.6 convert.2
  129.9 13.5 %all-to-all-start.3 = ((bf16[64,1,3]{2,1,0:T(2,128)(2,1)}), bf16[64,1,3]{2,1,0:T(2,128)(2,1)S(1)}, u32[]{:S(2)}, u32[]{:S(2)}) async-start(bf16[64,1,3]{2,1,0:T(2,128)(2,1)} %convert.2), calls=%async_computation.4 | async-start | bytes 65536 | tf_op jit(solution)/shard_map/all_to_all | solution.py:228
  143.4 9.3 %all-to-all-done.3 = bf16[64,1,3]{2,1,0:T(2,128)(2,1)S(1)} async-done(((bf16[64,1,3]{2,1,0:T(2,128)(2,1)}), bf16[64,1,3]{2,1,0:T(2,128)(2,1)S(1)}, u32[]{:S(2)}, u32[]{:S(2)}) %all-to-all-start.3) | async-done | bytes 416 | tf_op jit(solution)/shard_map/all_to_all | solution.py:228
  153.1 0.4 convolution_bitcast_fusion
  153.8 1.5 reshape.116
  155.3 4.7 %all-to-all-start.4 = ((f32[64,1,2048]{2,1,0:T(1,128)}), f32[64,1,2048]{2,1,0:T(1,128)S(1)}, u32[]{:S(2)}, u32[]{:S(2)}) async-start(f32[64,1,2048]{2,1,0:T(1,128)} %reshape.116), calls=%async_computation.5 | async-start | bytes 1048576 | tf_op jit(solution)/shard_map/all_to_all | solution.py:245
  160.0 17.8 %all-to-all-done.4 = f32[64,1,2048]{2,1,0:T(1,128)S(1)} async-done(((f32[64,1,2048]{2,1,0:T(1,128)}), f32[64,1,2048]{2,1,0:T(1,128)S(1)}, u32[]{:S(2)}, u32[]{:S(2)}) %all-to-all-start.4) | async-done | bytes 524320 | tf_op jit(solution)/shard_map/all_to_all | solution.py:245
  177.8 0.5 broadcast.116
  178.4 1.9 reduce.3
  180.3 0.4 reshape.117
  180.8 0.7 reshape.118
  181.5 3.6 %all-to-all-start.5 = ((f32[8,1,256]{2,1,0:T(1,128)}), f32[8,1,256]{2,1,0:T(1,128)S(1)}, u32[]{:S(2)}, u32[]{:S(2)}) async-start(f32[8,1,256]{2,1,0:T(1,128)} %reshape.118), calls=%async_computation.6 | async-start | bytes 16384 | tf_op jit(solution)/shard_map/all_to_all | solution.py:247
  185.1 0.4 fusion.14
  185.5 6.5 %all-to-all-done.5 = f32[8,1,256]{2,1,0:T(1,128)S(1)} async-done(((f32[8,1,256]{2,1,0:T(1,128)}), f32[8,1,256]{2,1,0:T(1,128)S(1)}, u32[]{:S(2)}, u32[]{:S(2)}) %all-to-all-start.5) | async-done | bytes 8224 | tf_op jit(solution)/shard_map/all_to_all | solution.py:247
  192.0 0.7 reduce.4
  192.7 0.6 reduce_sum.79
  193.3 1.3 reduce-scatter.2.cloned.1.call-done
  194.7 1.4 reshape.107
  196.1 32.9 %all_to_all.36 = bf16[64,48,128]{2,1,0:T(8,128)(2,1)S(1)} all-to-all(bf16[64,48,128]{2,1,0:T(8,128)(2,1)S(1)} %reshape.107), channel_id=1, replica_groups=mesh['expert'=64,'dp'=8] {'expert'}, dimensions={0} | all-to-all | bytes 1572864 | tf_op jit(solution)/shard_map/all_to_all | solution.py:254
  229.0 0.3 reshape.108
  229.4 1.1 fusion.2
  (41 shorter events, 1.9 us)
Async XLA Ops:
  7.2 10.0 %copy-start = (bf16[128,2048]{1,0:T(8,128)(2,1)S(1)}, bf16[128,2048]{1,0:T(8,128)(2,1)}, u32[]{:S(2)}) copy-start(bf16[128,2048]{1,0:T(8,128)(2,1)} %param.13) | copy-start | bytes 1572868
  7.2 81.4 %all-gather.3.cloned.1.call-start = ((), (), s32[]{:S(2)}) async-start(), calls=%async_computation.9 | async-start | bytes 6488064 | tf_op jit(solution)/shard_map/all_gather | solution.py:119
  18.9 12.0 %copy-start.5 = (bf16[1,64,8,3,2,176]{5,4,3,2,1,0:T(2,128)(2,1)S(1)}, bf16[1,64,8,3,2,176]{5,4,3,2,1,0:T(2,128)(2,1)}, u32[]{:S(2)}) copy-start(bf16[1,64,8,3,2,176]{5,4,3,2,1,0:T(2,128)(2,1)} %param.20) | copy-start | bytes 3244036
  18.9 39.9 %all-to-all-start = ((bf16[64,4,2048]{2,1,0:T(4,128)(2,1)}), bf16[64,4,2048]{2,1,0:T(4,128)(2,1)}, u32[]{:S(2)}, u32[]{:S(2)}) async-start(bf16[64,4,2048]{2,1,0:T(4,128)(2,1)} %reshape.101), calls=%async_computation | async-start | bytes 2097152 | tf_op jit(solution)/shard_map/all_to_all | solution.py:147
  30.8 163.9 %reduce-scatter.2.cloned.1.call-start = ((), (), s32[]{:S(2)}) async-start(), calls=%async_computation.8 | async-start | bytes 7077888 | tf_op jit(solution)/shard_map/reduce_scatter | solution.py:211
  88.6 24.1 %copy-start.1 = (f32[8,176,192]{2,1,0:T(8,128)S(1)}, f32[8,176,192]{2,1,0:T(8,128)}, u32[]{:S(2)}) copy-start(f32[8,176,192]{2,1,0:T(8,128)} %get-tuple-element.18.scale_a_ref) | copy-start | bytes 3244036
  88.6 24.1 %copy-start.2 = (f32[8,176,192]{2,1,0:T(8,128)S(1)}, f32[8,176,192]{2,1,0:T(8,128)}, u32[]{:S(2)}) copy-start(f32[8,176,192]{2,1,0:T(8,128)} %get-tuple-element.19.scale_b_ref) | copy-start | bytes 3244036
  88.6 24.1 %copy-start.3 = (bf16[1,2048,176]{1,2,0:T(8,128)(2,1)S(1)}, bf16[1,2048,176]{1,2,0:T(8,128)(2,1)}, u32[]{:S(2)}) copy-start(bf16[1,2048,176]{1,2,0:T(8,128)(2,1)} %param.17) | copy-start | bytes 2162692
  88.6 24.1 %copy-start.4 = (bf16[1,2048,176]{1,2,0:T(8,128)(2,1)S(1)}, bf16[1,2048,176]{1,2,0:T(8,128)(2,1)}, u32[]{:S(2)}) copy-start(bf16[1,2048,176]{1,2,0:T(8,128)(2,1)} %param.18) | copy-start | bytes 2162692
  117.9 0.8 copy-start.8
  117.9 1.1 copy-start.9
  117.9 35.2 %copy-start.6 = (bf16[128,2048]{1,0:T(8,128)(2,1)S(1)}, bf16[128,2048]{1,0:T(8,128)(2,1)}, u32[]{:S(2)}) copy-start(bf16[128,2048]{1,0:T(8,128)(2,1)} %param.12) | copy-start | bytes 1572868
  119.2 9.9 %all-to-all-start.2 = ((f32[8,1,192]{2,1,0:T(1,128)}), f32[8,1,192]{2,1,0:T(1,128)S(1)}, u32[]{:S(2)}, u32[]{:S(2)}) async-start(f32[8,1,192]{2,1,0:T(1,128)} %get-tuple-element.22), calls=%async_computation.3 | async-start | bytes 16384 | tf_op jit(solution)/shard_map/all_to_all | solution.py:226
  129.9 22.8 %all-to-all-start.3 = ((bf16[64,1,3]{2,1,0:T(2,128)(2,1)}), bf16[64,1,3]{2,1,0:T(2,128)(2,1)S(1)}, u32[]{:S(2)}, u32[]{:S(2)}) async-start(bf16[64,1,3]{2,1,0:T(2,128)(2,1)} %convert.2), calls=%async_computation.4 | async-start | bytes 65536 | tf_op jit(solution)/shard_map/all_to_all | solution.py:228
  155.3 22.6 %all-to-all-start.4 = ((f32[64,1,2048]{2,1,0:T(1,128)}), f32[64,1,2048]{2,1,0:T(1,128)S(1)}, u32[]{:S(2)}, u32[]{:S(2)}) async-start(f32[64,1,2048]{2,1,0:T(1,128)} %reshape.116), calls=%async_computation.5 | async-start | bytes 1048576 | tf_op jit(solution)/shard_map/all_to_all | solution.py:245
  180.2 4.9 %copy-start.7 = (bf16[64,2048]{1,0:T(8,128)(2,1)S(1)}, bf16[64,2048]{1,0:T(8,128)(2,1)}, u32[]{:S(2)}) copy-start(bf16[64,2048]{1,0:T(8,128)(2,1)} %param.16) | copy-start | bytes 786436
  181.5 10.5 %all-to-all-start.5 = ((f32[8,1,256]{2,1,0:T(1,128)}), f32[8,1,256]{2,1,0:T(1,128)S(1)}, u32[]{:S(2)}, u32[]{:S(2)}) async-start(f32[8,1,256]{2,1,0:T(1,128)} %reshape.118), calls=%async_computation.6 | async-start | bytes 16384 | tf_op jit(solution)/shard_map/all_to_all | solution.py:247
Sparse Core Ops, SparseCore 0:
  10.1 78.4 all-gather.2
  118.1 76.5 reduce-scatter.1

commit v6 on v5

--- a/solution.py
+++ b/solution.py
@@ -241,9 +241,13 @@
 
     router_part = jnp.einsum("td,te->de", layer_input, logit_grad, preferred_element_type=f32)
     share = width // expert_count
-    router_part = router_part.reshape(expert_count, share, experts)
+    router_part = router_part.reshape(expert_count, 2, share // 2, experts)
+    router_part = jnp.concatenate([router_part[:, 0], router_part[:, 1]], axis=2)
     router_part = lax.all_to_all(router_part, "expert", split_axis=0, concat_axis=0, tiled=True)
-    router_part = jnp.sum(router_part, axis=0).reshape(dp_count, share // dp_count, experts)
+    router_part = jnp.sum(router_part, axis=0)
+    router_part = jnp.concatenate(
+        [router_part[:, :experts], router_part[:, experts:]], axis=0
+    ).reshape(dp_count, share // dp_count, experts)
     router_part = lax.all_to_all(router_part, "dp", split_axis=0, concat_axis=0, tiled=True)
     router_grad = jnp.sum(router_part, axis=0).T
 

time: 238 us -> 238 us (level)
  waiting for transfers between devices: 78.8 us -> 81.5 us
    reduce_scatter x1, waiting for transfers between devices: 1.35 us -> 3.97 us  [local(): lax.psum_scatter(part.reshape(dp_count * rows, width), 'dp', scatter_dime...]
  transfers between devices with their start and end apart: 7 -> 7, of which waited for: 7 -> 7; matrix products, arithmetic and copies ran while one was open for 14% -> 13% of each run, Pallas kernels for 0% -> 0%
where the time goes in v6:
time: 238 us; the launch traced here: 237 us
  waiting for transfers between devices  81.5 us (34%)
  blocking collectives  53 us (22%)
  starting transfers between devices  37.3 us (16%)
  between operations  21.8 us (9%)
  local copies, waits for them, and re-layouts  16.9 us (7%)
  other arithmetic  15.4 us (6%)
  Pallas kernels  9.08 us (4%)
  matrix products  2.42 us (1%)
    all_to_all x1, blocking collectives, local(): lax.all_to_all(routed.reshape(expert_count, rows * width // expert_count...  32.9 us
    all_gather x1, waiting for transfers between devices, local(): down_full = lax.all_gather(down_weight[0], 'dp', axis=0, tiled=True)  26.6 us
    all_to_all x1, blocking collectives, local(): lax.all_to_all(packed, 'dp', split_axis=0, concat_axis=0, tiled=True)  20.1 us
    all_to_all x1, waiting for transfers between devices, local(): lax.all_to_all(router_part, 'expert', split_axis=0, concat_axis=0, tiled=...  17.8 us
    all_to_all x1, waiting for transfers between devices, local(): lax.all_to_all(outgoing, 'expert', split_axis=0, concat_axis=0, tiled=True)  14.6 us
    all_to_all x1, starting transfers between devices, local(): lax.all_to_all(gate_sum, 'expert', split_axis=0, concat_axis=0, tiled=True)  13.5 us
    all_to_all x1, starting transfers between devices, local(): lax.all_to_all(outgoing, 'expert', split_axis=0, concat_axis=0, tiled=True)  11.9 us
    all_to_all x1, waiting for transfers between devices, local(): lax.all_to_all(gate_sum, 'expert', split_axis=0, concat_axis=0, tiled=True)  9.29 us
  transfers between devices with their start and end apart: 7, of which 7 were waited for; matrix products, arithmetic and copies ran while one was open for 13% of the time, Pallas kernels for 0%

profile of v6, /device:TPU:1, one launch (start us, length us, event | category | flops | bytes accessed | tf_op | source)
XLA Modules:
  0.0 237.3 jit_solution(7524839406816356926)
XLA Ops:
  7.2 0.7 all-gather.3.cloned.1.call-update
  12.8 0.7 fusion.7
  13.8 1.9 select_select_fusion
  15.7 0.8 select_reduce_fusion
  16.5 0.7 multiply_add_fusion
  17.2 0.4 fusion
  17.6 1.2 reshape.101
  18.9 11.9 %all-to-all-start = ((bf16[64,4,2048]{2,1,0:T(4,128)(2,1)}), bf16[64,4,2048]{2,1,0:T(4,128)(2,1)}, u32[]{:S(2)}, u32[]{:S(2)}) async-start(bf16[64,4,2048]{2,1,0:T(4,128)(2,1)} %reshape.101), calls=%async_computation | async-start | bytes 2097152 | tf_op jit(solution)/shard_map/all_to_all | solution.py:147
  30.9 0.5 copy.114
  31.4 1.5 slice_convert_fusion.1
  32.9 0.9 copy.90
  33.8 1.9 copy.91
  35.7 2.3 copy.89
  38.0 1.9 copy.92
  39.9 4.2 %fusion.15 = (f32[8,176,192]{2,1,0:T(8,128)S(1)}, f32[8,176,192]{2,1,0:T(8,128)}, f32[8,176,192]{2,1,0:T(8,128)}) fusion(f32[8,176,192]{2,1,0:T(8,128)} %copy.92, f32[8,176,192]{2,1,0:T(8,128)} %copy.91), kind=kLoop, calls=%fused_computation.55 | loop fusion | flops 2703360 | bytes 5406720 | tf_op jit(solution)/shard_map/mul | solution.py:156
  44.2 14.6 %all-to-all-done = bf16[64,4,2048]{2,1,0:T(4,128)(2,1)} async-done(((bf16[64,4,2048]{2,1,0:T(4,128)(2,1)}), bf16[64,4,2048]{2,1,0:T(4,128)(2,1)}, u32[]{:S(2)}, u32[]{:S(2)}) %all-to-all-start) | async-done | bytes 1048608 | tf_op jit(solution)/shard_map/all_to_all | solution.py:147
  58.7 2.4 %reshape.102.refs_4_ = bf16[192,2048]{1,0:T(8,128)(2,1)S(1)} reshape(bf16[64,3,2048]{2,1,0:T(4,128)(2,1)} %bitcast.62) | data formatting | bytes 1572864 | tf_op jit(solution)/shard_map/reshape | solution.py:148
  61.1 0.9 slice.63
  62.0 26.6 %all-gather.3.cloned.1.call-done = bf16[1,1408,2048]{2,1,0:T(8,128)(2,1)} async-done(((bf16[1,176,2048]{2,1,0:T(8,128)(2,1)}), bf16[1,1408,2048]{2,1,0:T(8,128)(2,1)}) %all-gather.3.cloned.1.call-update) | async-done | bytes 5767184 | tf_op jit(solution)/shard_map/all_gather | solution.py:119
  88.6 4.0 %shard_map.131 = bf16[8,272,128]{2,1,0:T(8,128)(2,1)S(1)} custom-call(bf16[1408,2048]{1,0:T(8,128)(2,1)} %bitcast.74, bf16[1408,2048]{1,0:T(8,128)(2,1)} %bitcast.75, bf16[1408,2048]{1,0:T(8,128)(2,1)} %bitcast.76, bf16[1408,2048]{1,0:T(8,128)(2,1)} %bitcast.77, bf16[192,2048]{1,0:T(8,128)(2,1)S(1)} %reshape.102.refs_4_, bf16[64,128]{1,0:T(8,128)(2,1)S(1)} %bitcast.71), custom_call_target="tpu_custom_call" | custom-call | flops 1107296256 | bytes 5767168 | tf_op jit(solution)/shard_map/pallas_call | solution.py:163
  92.6 20.1 %all_to_all.35.packed_ref = bf16[8,272,128]{2,1,0:T(8,128)(2,1)S(1)} all-to-all(bf16[8,272,128]{2,1,0:T(8,128)(2,1)S(1)} %shard_map.131), channel_id=1, replica_groups=mesh['expert'=64,'dp'=8] {'dp'}, dimensions={0} | all-to-all | bytes 1114112 | tf_op jit(solution)/shard_map/all_to_all | solution.py:187
  112.8 5.1 %shard_map.132 = (bf16[8,192,2048]{2,1,0:T(8,128)(2,1)}, f32[8,1,192]{2,1,0:T(1,128)}) custom-call(bf16[8,272,128]{2,1,0:T(8,128)(2,1)S(1)} %all_to_all.35.packed_ref, f32[8,176,192]{2,1,0:T(8,128)S(1)} %copy-done.1, f32[8,176,192]{2,1,0:T(8,128)S(1)} %copy-done.2, f32[8,176,192]{2,1,0:T(8,128)S(1)} %get-tuple-element.20.scale_g_ref, ...), custom_call_target="tpu_custom_call" | custom-call | flops 2214592512 | bytes 6291456 | tf_op jit(solution)/shard_map/pallas_call | solution.py:189
  117.9 0.7 copy-done.8
  119.0 0.2 multiply_reduce_fusion
  119.2 3.3 %all-to-all-start.2 = ((f32[8,1,192]{2,1,0:T(1,128)}), f32[8,1,192]{2,1,0:T(1,128)S(1)}, u32[]{:S(2)}, u32[]{:S(2)}) async-start(f32[8,1,192]{2,1,0:T(1,128)} %get-tuple-element.22), calls=%async_computation.3 | async-start | bytes 16384 | tf_op jit(solution)/shard_map/all_to_all | solution.py:226
  122.6 0.6 fusion.16
  123.2 1.3 multiply_reduce_fusion.1
  127.0 2.1 all-to-all-done.2
  129.2 0.6 convert.2
  129.9 13.5 %all-to-all-start.3 = ((bf16[64,1,3]{2,1,0:T(2,128)(2,1)}), bf16[64,1,3]{2,1,0:T(2,128)(2,1)S(1)}, u32[]{:S(2)}, u32[]{:S(2)}) async-start(bf16[64,1,3]{2,1,0:T(2,128)(2,1)} %convert.2), calls=%async_computation.4 | async-start | bytes 65536 | tf_op jit(solution)/shard_map/all_to_all | solution.py:228
  143.4 9.3 %all-to-all-done.3 = bf16[64,1,3]{2,1,0:T(2,128)(2,1)S(1)} async-done(((bf16[64,1,3]{2,1,0:T(2,128)(2,1)}), bf16[64,1,3]{2,1,0:T(2,128)(2,1)S(1)}, u32[]{:S(2)}, u32[]{:S(2)}) %all-to-all-start.3) | async-done | bytes 416 | tf_op jit(solution)/shard_map/all_to_all | solution.py:228
  153.1 0.4 convolution_bitcast_fusion
  153.5 0.3 copy.102
  153.9 1.0 pad_maximum_fusion
  154.9 4.7 %all-to-all-start.4 = ((f32[64,16,128]{2,1,0:T(8,128)}), f32[64,16,128]{2,1,0:T(8,128)S(1)}, u32[]{:S(2)}, u32[]{:S(2)}) async-start(f32[64,16,128]{2,1,0:T(8,128)} %pad_maximum_fusion), calls=%async_computation.5 | async-start | bytes 1048576 | tf_op jit(solution)/shard_map/all_to_all | solution.py:246
  159.7 17.8 %all-to-all-done.4 = f32[64,16,128]{2,1,0:T(8,128)S(1)} async-done(((f32[64,16,128]{2,1,0:T(8,128)}), f32[64,16,128]{2,1,0:T(8,128)S(1)}, u32[]{:S(2)}, u32[]{:S(2)}) %all-to-all-start.4) | async-done | bytes 524320 | tf_op jit(solution)/shard_map/all_to_all | solution.py:246
  177.6 0.7 reshape.116
  178.3 3.6 %all-to-all-start.5 = ((f32[8,1,256]{2,1,0:T(1,128)}), f32[8,1,256]{2,1,0:T(1,128)S(1)}, u32[]{:S(2)}, u32[]{:S(2)}) async-start(f32[8,1,256]{2,1,0:T(1,128)} %reshape.116), calls=%async_computation.6 | async-start | bytes 16384 | tf_op jit(solution)/shard_map/all_to_all | solution.py:251
  182.0 0.4 fusion.14
  182.3 6.5 %all-to-all-done.5 = f32[8,1,256]{2,1,0:T(1,128)S(1)} async-done(((f32[8,1,256]{2,1,0:T(1,128)}), f32[8,1,256]{2,1,0:T(1,128)S(1)}, u32[]{:S(2)}, u32[]{:S(2)}) %all-to-all-start.5) | async-done | bytes 8224 | tf_op jit(solution)/shard_map/all_to_all | solution.py:251
  188.8 0.5 broadcast.116
  189.4 0.7 reduce.3
  190.1 0.6 reduce_sum.79
  190.7 4.0 %reduce-scatter.2.cloned.1.call-done = bf16[192,2048]{1,0:T(8,128)(2,1)} async-done(((bf16[1536,2048]{1,0:T(8,128)(2,1)}), bf16[192,2048]{1,0:T(8,128)(2,1)}) %reduce-scatter.2.cloned.1.call-update) | async-done | bytes 786448 | tf_op jit(solution)/shard_map/reduce_scatter | solution.py:211
  194.7 1.4 reshape.107
  196.1 32.9 %all_to_all.36 = bf16[64,48,128]{2,1,0:T(8,128)(2,1)S(1)} all-to-all(bf16[64,48,128]{2,1,0:T(8,128)(2,1)S(1)} %reshape.107), channel_id=1, replica_groups=mesh['expert'=64,'dp'=8] {'expert'}, dimensions={0} | all-to-all | bytes 1572864 | tf_op jit(solution)/shard_map/all_to_all | solution.py:258
  229.0 0.3 reshape.108
  229.4 1.1 fusion.2
  (42 shorter events, 1.5 us)
Async XLA Ops:
  7.2 10.0 %copy-start = (bf16[128,2048]{1,0:T(8,128)(2,1)S(1)}, bf16[128,2048]{1,0:T(8,128)(2,1)}, u32[]{:S(2)}) copy-start(bf16[128,2048]{1,0:T(8,128)(2,1)} %param.13) | copy-start | bytes 1572868
  7.2 81.4 %all-gather.3.cloned.1.call-start = ((), (), s32[]{:S(2)}) async-start(), calls=%async_computation.9 | async-start | bytes 6488064 | tf_op jit(solution)/shard_map/all_gather | solution.py:119
  18.9 12.0 %copy-start.5 = (bf16[1,64,8,3,2,176]{5,4,3,2,1,0:T(2,128)(2,1)S(1)}, bf16[1,64,8,3,2,176]{5,4,3,2,1,0:T(2,128)(2,1)}, u32[]{:S(2)}) copy-start(bf16[1,64,8,3,2,176]{5,4,3,2,1,0:T(2,128)(2,1)} %param.20) | copy-start | bytes 3244036
  18.9 39.9 %all-to-all-start = ((bf16[64,4,2048]{2,1,0:T(4,128)(2,1)}), bf16[64,4,2048]{2,1,0:T(4,128)(2,1)}, u32[]{:S(2)}, u32[]{:S(2)}) async-start(bf16[64,4,2048]{2,1,0:T(4,128)(2,1)} %reshape.101), calls=%async_computation | async-start | bytes 2097152 | tf_op jit(solution)/shard_map/all_to_all | solution.py:147
  30.8 163.9 %reduce-scatter.2.cloned.1.call-start = ((), (), s32[]{:S(2)}) async-start(), calls=%async_computation.8 | async-start | bytes 7077888 | tf_op jit(solution)/shard_map/reduce_scatter | solution.py:211
  88.6 24.1 %copy-start.1 = (f32[8,176,192]{2,1,0:T(8,128)S(1)}, f32[8,176,192]{2,1,0:T(8,128)}, u32[]{:S(2)}) copy-start(f32[8,176,192]{2,1,0:T(8,128)} %get-tuple-element.18.scale_a_ref) | copy-start | bytes 3244036
  88.6 24.1 %copy-start.2 = (f32[8,176,192]{2,1,0:T(8,128)S(1)}, f32[8,176,192]{2,1,0:T(8,128)}, u32[]{:S(2)}) copy-start(f32[8,176,192]{2,1,0:T(8,128)} %get-tuple-element.19.scale_b_ref) | copy-start | bytes 3244036
  88.6 24.1 %copy-start.3 = (bf16[1,2048,176]{1,2,0:T(8,128)(2,1)S(1)}, bf16[1,2048,176]{1,2,0:T(8,128)(2,1)}, u32[]{:S(2)}) copy-start(bf16[1,2048,176]{1,2,0:T(8,128)(2,1)} %param.17) | copy-start | bytes 2162692
  88.6 24.1 %copy-start.4 = (bf16[1,2048,176]{1,2,0:T(8,128)(2,1)S(1)}, bf16[1,2048,176]{1,2,0:T(8,128)(2,1)}, u32[]{:S(2)}) copy-start(bf16[1,2048,176]{1,2,0:T(8,128)(2,1)} %param.18) | copy-start | bytes 2162692
  117.9 0.8 copy-start.8
  117.9 1.1 copy-start.9
  117.9 35.2 %copy-start.6 = (bf16[128,2048]{1,0:T(8,128)(2,1)S(1)}, bf16[128,2048]{1,0:T(8,128)(2,1)}, u32[]{:S(2)}) copy-start(bf16[128,2048]{1,0:T(8,128)(2,1)} %param.12) | copy-start | bytes 1572868
  119.2 9.9 %all-to-all-start.2 = ((f32[8,1,192]{2,1,0:T(1,128)}), f32[8,1,192]{2,1,0:T(1,128)S(1)}, u32[]{:S(2)}, u32[]{:S(2)}) async-start(f32[8,1,192]{2,1,0:T(1,128)} %get-tuple-element.22), calls=%async_computation.3 | async-start | bytes 16384 | tf_op jit(solution)/shard_map/all_to_all | solution.py:226
  129.9 22.8 %all-to-all-start.3 = ((bf16[64,1,3]{2,1,0:T(2,128)(2,1)}), bf16[64,1,3]{2,1,0:T(2,128)(2,1)S(1)}, u32[]{:S(2)}, u32[]{:S(2)}) async-start(bf16[64,1,3]{2,1,0:T(2,128)(2,1)} %convert.2), calls=%async_computation.4 | async-start | bytes 65536 | tf_op jit(solution)/shard_map/all_to_all | solution.py:228
  153.9 28.1 %copy-start.7 = (bf16[64,2048]{1,0:T(8,128)(2,1)S(1)}, bf16[64,2048]{1,0:T(8,128)(2,1)}, u32[]{:S(2)}) copy-start(bf16[64,2048]{1,0:T(8,128)(2,1)} %param.16) | copy-start | bytes 786436
  154.9 22.6 %all-to-all-start.4 = ((f32[64,16,128]{2,1,0:T(8,128)}), f32[64,16,128]{2,1,0:T(8,128)S(1)}, u32[]{:S(2)}, u32[]{:S(2)}) async-start(f32[64,16,128]{2,1,0:T(8,128)} %pad_maximum_fusion), calls=%async_computation.5 | async-start | bytes 1048576 | tf_op jit(solution)/shard_map/all_to_all | solution.py:246
  178.3 10.5 %all-to-all-start.5 = ((f32[8,1,256]{2,1,0:T(1,128)}), f32[8,1,256]{2,1,0:T(1,128)S(1)}, u32[]{:S(2)}, u32[]{:S(2)}) async-start(f32[8,1,256]{2,1,0:T(1,128)} %reshape.116), calls=%async_computation.6 | async-start | bytes 16384 | tf_op jit(solution)/shard_map/all_to_all | solution.py:251
Sparse Core Ops, SparseCore 0:
  10.1 78.4 all-gather.2
  118.1 76.5 reduce-scatter.1

commit v7 on v6

--- a/solution.py
+++ b/solution.py
@@ -12,7 +12,7 @@
 RECORD_ROWS = 8
 DOWN_PIECES = 4
 DOWN_HOLDERS = 4
-UP_CHUNKS = 2
+UP_CHUNKS = 1
 VMEM_GRANT = 32 * 2**20
 
 
@@ -70,8 +70,8 @@
         tail = jnp.concatenate([tail[:, :seam], tail[:, seam:]], axis=0)
         down_grad = jnp.concatenate([head, tail], axis=1)
         gate_part_ref[sender] = jnp.sum(down_grad * scale_g_ref[sender], axis=0, keepdims=True)
-        grad_a = jnp.transpose(down_grad * scale_a_ref[sender]).astype(bf16)
-        grad_b = jnp.transpose(down_grad * scale_b_ref[sender]).astype(bf16)
+        grad_a = jnp.transpose((down_grad * scale_a_ref[sender]).astype(bf16))
+        grad_b = jnp.transpose((down_grad * scale_b_ref[sender]).astype(bf16))
         for chunk in range(UP_CHUNKS):
             columns = slice(chunk * span, (chunk + 1) * span)
             part = jnp.dot(grad_a, gate_ref[:, columns], preferred_element_type=f32)

time: 238 us -> 238 us (level)
  no operation moved by 1% of the time
where the time goes in v7:
time: 238 us; the launch traced here: 237 us
  waiting for transfers between devices  81.3 us (34%)
  blocking collectives  53 us (22%)
  starting transfers between devices  37.5 us (16%)
  between operations  21.8 us (9%)
  local copies, waits for them, and re-layouts  16.9 us (7%)
  other arithmetic  15.4 us (6%)
  Pallas kernels  9.09 us (4%)
  matrix products  2.44 us (1%)
    all_to_all x1, blocking collectives, local(): lax.all_to_all(routed.reshape(expert_count, rows * width // expert_count...  32.9 us
    all_gather x1, waiting for transfers between devices, local(): down_full = lax.all_gather(down_weight[0], 'dp', axis=0, tiled=True)  26.6 us
    all_to_all x1, blocking collectives, local(): lax.all_to_all(packed, 'dp', split_axis=0, concat_axis=0, tiled=True)  20.1 us
    all_to_all x1, waiting for transfers between devices, local(): lax.all_to_all(router_part, 'expert', split_axis=0, concat_axis=0, tiled=...  17.8 us
    all_to_all x1, waiting for transfers between devices, local(): lax.all_to_all(outgoing, 'expert', split_axis=0, concat_axis=0, tiled=True)  14.6 us
    all_to_all x1, starting transfers between devices, local(): lax.all_to_all(gate_sum, 'expert', split_axis=0, concat_axis=0, tiled=True)  13.6 us
    all_to_all x1, starting transfers between devices, local(): lax.all_to_all(outgoing, 'expert', split_axis=0, concat_axis=0, tiled=True)  11.9 us
    all_to_all x1, waiting for transfers between devices, local(): lax.all_to_all(gate_sum, 'expert', split_axis=0, concat_axis=0, tiled=True)  9.29 us
  transfers between devices with their start and end apart: 7, of which 7 were waited for; matrix products, arithmetic and copies ran while one was open for 13% of the time, Pallas kernels for 0%

profile of v7, /device:TPU:1, one launch (start us, length us, event | category | flops | bytes accessed | tf_op | source)
XLA Modules:
  0.0 237.3 jit_solution(9682637521679963538)
XLA Ops:
  7.2 0.7 all-gather.3.cloned.1.call-update
  12.8 0.7 fusion.7
  13.8 1.9 select_select_fusion
  15.7 0.8 select_reduce_fusion
  16.5 0.7 multiply_add_fusion
  17.2 0.4 fusion
  17.6 1.2 reshape.101
  18.9 11.9 %all-to-all-start = ((bf16[64,4,2048]{2,1,0:T(4,128)(2,1)}), bf16[64,4,2048]{2,1,0:T(4,128)(2,1)}, u32[]{:S(2)}, u32[]{:S(2)}) async-start(bf16[64,4,2048]{2,1,0:T(4,128)(2,1)} %reshape.101), calls=%async_computation | async-start | bytes 2097152 | tf_op jit(solution)/shard_map/all_to_all | solution.py:147
  30.9 0.5 copy.114
  31.4 1.5 slice_convert_fusion.1
  32.9 0.9 copy.90
  33.8 1.9 copy.91
  35.7 2.3 copy.89
  38.0 1.9 copy.92
  39.9 4.2 %fusion.15 = (f32[8,176,192]{2,1,0:T(8,128)S(1)}, f32[8,176,192]{2,1,0:T(8,128)}, f32[8,176,192]{2,1,0:T(8,128)}) fusion(f32[8,176,192]{2,1,0:T(8,128)} %copy.92, f32[8,176,192]{2,1,0:T(8,128)} %copy.91), kind=kLoop, calls=%fused_computation.55 | loop fusion | flops 2703360 | bytes 5406720 | tf_op jit(solution)/shard_map/mul | solution.py:156
  44.2 14.6 %all-to-all-done = bf16[64,4,2048]{2,1,0:T(4,128)(2,1)} async-done(((bf16[64,4,2048]{2,1,0:T(4,128)(2,1)}), bf16[64,4,2048]{2,1,0:T(4,128)(2,1)}, u32[]{:S(2)}, u32[]{:S(2)}) %all-to-all-start) | async-done | bytes 1048608 | tf_op jit(solution)/shard_map/all_to_all | solution.py:147
  58.7 2.4 %reshape.102.refs_4_ = bf16[192,2048]{1,0:T(8,128)(2,1)S(1)} reshape(bf16[64,3,2048]{2,1,0:T(4,128)(2,1)} %bitcast.62) | data formatting | bytes 1572864 | tf_op jit(solution)/shard_map/reshape | solution.py:148
  61.1 0.9 slice.63
  62.0 26.6 %all-gather.3.cloned.1.call-done = bf16[1,1408,2048]{2,1,0:T(8,128)(2,1)} async-done(((bf16[1,176,2048]{2,1,0:T(8,128)(2,1)}), bf16[1,1408,2048]{2,1,0:T(8,128)(2,1)}) %all-gather.3.cloned.1.call-update) | async-done | bytes 5767184 | tf_op jit(solution)/shard_map/all_gather | solution.py:119
  88.6 4.0 %shard_map.131 = bf16[8,272,128]{2,1,0:T(8,128)(2,1)S(1)} custom-call(bf16[1408,2048]{1,0:T(8,128)(2,1)} %bitcast.74, bf16[1408,2048]{1,0:T(8,128)(2,1)} %bitcast.75, bf16[1408,2048]{1,0:T(8,128)(2,1)} %bitcast.76, bf16[1408,2048]{1,0:T(8,128)(2,1)} %bitcast.77, bf16[192,2048]{1,0:T(8,128)(2,1)S(1)} %reshape.102.refs_4_, bf16[64,128]{1,0:T(8,128)(2,1)S(1)} %bitcast.71), custom_call_target="tpu_custom_call" | custom-call | flops 1107296256 | bytes 5767168 | tf_op jit(solution)/shard_map/pallas_call | solution.py:163
  92.6 20.1 %all_to_all.35.packed_ref = bf16[8,272,128]{2,1,0:T(8,128)(2,1)S(1)} all-to-all(bf16[8,272,128]{2,1,0:T(8,128)(2,1)S(1)} %shard_map.131), channel_id=1, replica_groups=mesh['expert'=64,'dp'=8] {'dp'}, dimensions={0} | all-to-all | bytes 1114112 | tf_op jit(solution)/shard_map/all_to_all | solution.py:187
  112.8 5.1 %shard_map.132 = (bf16[8,192,2048]{2,1,0:T(8,128)(2,1)}, f32[8,1,192]{2,1,0:T(1,128)}) custom-call(bf16[8,272,128]{2,1,0:T(8,128)(2,1)S(1)} %all_to_all.35.packed_ref, f32[8,176,192]{2,1,0:T(8,128)S(1)} %copy-done.1, f32[8,176,192]{2,1,0:T(8,128)S(1)} %copy-done.2, f32[8,176,192]{2,1,0:T(8,128)S(1)} %get-tuple-element.20.scale_g_ref, ...), custom_call_target="tpu_custom_call" | custom-call | flops 2214592512 | bytes 6291456 | tf_op jit(solution)/shard_map/pallas_call | solution.py:189
  118.0 0.7 copy-done.8
  119.0 0.2 multiply_reduce_fusion
  119.2 3.5 %all-to-all-start.2 = ((f32[8,1,192]{2,1,0:T(1,128)}), f32[8,1,192]{2,1,0:T(1,128)S(1)}, u32[]{:S(2)}, u32[]{:S(2)}) async-start(f32[8,1,192]{2,1,0:T(1,128)} %get-tuple-element.22), calls=%async_computation.3 | async-start | bytes 16384 | tf_op jit(solution)/shard_map/all_to_all | solution.py:226
  122.7 0.6 fusion.16
  123.4 1.3 multiply_reduce_fusion.1
  127.2 1.9 all-to-all-done.2
  129.2 0.6 convert.2
  129.8 13.6 %all-to-all-start.3 = ((bf16[64,1,3]{2,1,0:T(2,128)(2,1)}), bf16[64,1,3]{2,1,0:T(2,128)(2,1)S(1)}, u32[]{:S(2)}, u32[]{:S(2)}) async-start(bf16[64,1,3]{2,1,0:T(2,128)(2,1)} %convert.2), calls=%async_computation.4 | async-start | bytes 65536 | tf_op jit(solution)/shard_map/all_to_all | solution.py:228
  143.4 9.3 %all-to-all-done.3 = bf16[64,1,3]{2,1,0:T(2,128)(2,1)S(1)} async-done(((bf16[64,1,3]{2,1,0:T(2,128)(2,1)}), bf16[64,1,3]{2,1,0:T(2,128)(2,1)S(1)}, u32[]{:S(2)}, u32[]{:S(2)}) %all-to-all-start.3) | async-done | bytes 416 | tf_op jit(solution)/shard_map/all_to_all | solution.py:228
  153.1 0.4 convolution_bitcast_fusion
  153.5 0.3 copy.102
  153.9 1.0 pad_maximum_fusion
  154.9 4.7 %all-to-all-start.4 = ((f32[64,16,128]{2,1,0:T(8,128)}), f32[64,16,128]{2,1,0:T(8,128)S(1)}, u32[]{:S(2)}, u32[]{:S(2)}) async-start(f32[64,16,128]{2,1,0:T(8,128)} %pad_maximum_fusion), calls=%async_computation.5 | async-start | bytes 1048576 | tf_op jit(solution)/shard_map/all_to_all | solution.py:246
  159.7 17.8 %all-to-all-done.4 = f32[64,16,128]{2,1,0:T(8,128)S(1)} async-done(((f32[64,16,128]{2,1,0:T(8,128)}), f32[64,16,128]{2,1,0:T(8,128)S(1)}, u32[]{:S(2)}, u32[]{:S(2)}) %all-to-all-start.4) | async-done | bytes 524320 | tf_op jit(solution)/shard_map/all_to_all | solution.py:246
  177.7 0.7 reshape.116
  178.3 3.6 %all-to-all-start.5 = ((f32[8,1,256]{2,1,0:T(1,128)}), f32[8,1,256]{2,1,0:T(1,128)S(1)}, u32[]{:S(2)}, u32[]{:S(2)}) async-start(f32[8,1,256]{2,1,0:T(1,128)} %reshape.116), calls=%async_computation.6 | async-start | bytes 16384 | tf_op jit(solution)/shard_map/all_to_all | solution.py:251
  182.0 0.4 fusion.14
  182.4 6.5 %all-to-all-done.5 = f32[8,1,256]{2,1,0:T(1,128)S(1)} async-done(((f32[8,1,256]{2,1,0:T(1,128)}), f32[8,1,256]{2,1,0:T(1,128)S(1)}, u32[]{:S(2)}, u32[]{:S(2)}) %all-to-all-start.5) | async-done | bytes 8224 | tf_op jit(solution)/shard_map/all_to_all | solution.py:251
  188.9 0.5 broadcast.116
  189.4 0.7 reduce.3
  190.1 0.6 reduce_sum.79
  190.7 4.0 %reduce-scatter.2.cloned.1.call-done = bf16[192,2048]{1,0:T(8,128)(2,1)} async-done(((bf16[1536,2048]{1,0:T(8,128)(2,1)}), bf16[192,2048]{1,0:T(8,128)(2,1)}) %reduce-scatter.2.cloned.1.call-update) | async-done | bytes 786448 | tf_op jit(solution)/shard_map/reduce_scatter | solution.py:211
  194.7 1.4 reshape.107
  196.2 32.9 %all_to_all.36 = bf16[64,48,128]{2,1,0:T(8,128)(2,1)S(1)} all-to-all(bf16[64,48,128]{2,1,0:T(8,128)(2,1)S(1)} %reshape.107), channel_id=1, replica_groups=mesh['expert'=64,'dp'=8] {'expert'}, dimensions={0} | all-to-all | bytes 1572864 | tf_op jit(solution)/shard_map/all_to_all | solution.py:258
  229.0 0.3 reshape.108
  229.4 1.1 fusion.2
  (42 shorter events, 1.5 us)
Async XLA Ops:
  7.2 10.0 %copy-start = (bf16[128,2048]{1,0:T(8,128)(2,1)S(1)}, bf16[128,2048]{1,0:T(8,128)(2,1)}, u32[]{:S(2)}) copy-start(bf16[128,2048]{1,0:T(8,128)(2,1)} %param.13) | copy-start | bytes 1572868
  7.2 81.4 %all-gather.3.cloned.1.call-start = ((), (), s32[]{:S(2)}) async-start(), calls=%async_computation.9 | async-start | bytes 6488064 | tf_op jit(solution)/shard_map/all_gather | solution.py:119
  18.9 12.0 %copy-start.5 = (bf16[1,64,8,3,2,176]{5,4,3,2,1,0:T(2,128)(2,1)S(1)}, bf16[1,64,8,3,2,176]{5,4,3,2,1,0:T(2,128)(2,1)}, u32[]{:S(2)}) copy-start(bf16[1,64,8,3,2,176]{5,4,3,2,1,0:T(2,128)(2,1)} %param.20) | copy-start | bytes 3244036
  18.9 39.9 %all-to-all-start = ((bf16[64,4,2048]{2,1,0:T(4,128)(2,1)}), bf16[64,4,2048]{2,1,0:T(4,128)(2,1)}, u32[]{:S(2)}, u32[]{:S(2)}) async-start(bf16[64,4,2048]{2,1,0:T(4,128)(2,1)} %reshape.101), calls=%async_computation | async-start | bytes 2097152 | tf_op jit(solution)/shard_map/all_to_all | solution.py:147
  30.8 163.9 %reduce-scatter.2.cloned.1.call-start = ((), (), s32[]{:S(2)}) async-start(), calls=%async_computation.8 | async-start | bytes 7077888 | tf_op jit(solution)/shard_map/reduce_scatter | solution.py:211
  88.6 24.1 %copy-start.1 = (f32[8,176,192]{2,1,0:T(8,128)S(1)}, f32[8,176,192]{2,1,0:T(8,128)}, u32[]{:S(2)}) copy-start(f32[8,176,192]{2,1,0:T(8,128)} %get-tuple-element.18.scale_a_ref) | copy-start | bytes 3244036
  88.6 24.1 %copy-start.2 = (f32[8,176,192]{2,1,0:T(8,128)S(1)}, f32[8,176,192]{2,1,0:T(8,128)}, u32[]{:S(2)}) copy-start(f32[8,176,192]{2,1,0:T(8,128)} %get-tuple-element.19.scale_b_ref) | copy-start | bytes 3244036
  88.6 24.1 %copy-start.3 = (bf16[1,2048,176]{1,2,0:T(8,128)(2,1)S(1)}, bf16[1,2048,176]{1,2,0:T(8,128)(2,1)}, u32[]{:S(2)}) copy-start(bf16[1,2048,176]{1,2,0:T(8,128)(2,1)} %param.17) | copy-start | bytes 2162692
  88.6 24.1 %copy-start.4 = (bf16[1,2048,176]{1,2,0:T(8,128)(2,1)S(1)}, bf16[1,2048,176]{1,2,0:T(8,128)(2,1)}, u32[]{:S(2)}) copy-start(bf16[1,2048,176]{1,2,0:T(8,128)(2,1)} %param.18) | copy-start | bytes 2162692
  117.9 0.8 copy-start.8
  117.9 1.1 copy-start.9
  117.9 35.2 %copy-start.6 = (bf16[128,2048]{1,0:T(8,128)(2,1)S(1)}, bf16[128,2048]{1,0:T(8,128)(2,1)}, u32[]{:S(2)}) copy-start(bf16[128,2048]{1,0:T(8,128)(2,1)} %param.12) | copy-start | bytes 1572868
  119.2 9.8 %all-to-all-start.2 = ((f32[8,1,192]{2,1,0:T(1,128)}), f32[8,1,192]{2,1,0:T(1,128)S(1)}, u32[]{:S(2)}, u32[]{:S(2)}) async-start(f32[8,1,192]{2,1,0:T(1,128)} %get-tuple-element.22), calls=%async_computation.3 | async-start | bytes 16384 | tf_op jit(solution)/shard_map/all_to_all | solution.py:226
  129.8 22.9 %all-to-all-start.3 = ((bf16[64,1,3]{2,1,0:T(2,128)(2,1)}), bf16[64,1,3]{2,1,0:T(2,128)(2,1)S(1)}, u32[]{:S(2)}, u32[]{:S(2)}) async-start(bf16[64,1,3]{2,1,0:T(2,128)(2,1)} %convert.2), calls=%async_computation.4 | async-start | bytes 65536 | tf_op jit(solution)/shard_map/all_to_all | solution.py:228
  153.9 28.1 %copy-start.7 = (bf16[64,2048]{1,0:T(8,128)(2,1)S(1)}, bf16[64,2048]{1,0:T(8,128)(2,1)}, u32[]{:S(2)}) copy-start(bf16[64,2048]{1,0:T(8,128)(2,1)} %param.16) | copy-start | bytes 786436
  154.9 22.6 %all-to-all-start.4 = ((f32[64,16,128]{2,1,0:T(8,128)}), f32[64,16,128]{2,1,0:T(8,128)S(1)}, u32[]{:S(2)}, u32[]{:S(2)}) async-start(f32[64,16,128]{2,1,0:T(8,128)} %pad_maximum_fusion), calls=%async_computation.5 | async-start | bytes 1048576 | tf_op jit(solution)/shard_map/all_to_all | solution.py:246
  178.3 10.5 %all-to-all-start.5 = ((f32[8,1,256]{2,1,0:T(1,128)}), f32[8,1,256]{2,1,0:T(1,128)S(1)}, u32[]{:S(2)}, u32[]{:S(2)}) async-start(f32[8,1,256]{2,1,0:T(1,128)} %reshape.116), calls=%async_computation.6 | async-start | bytes 16384 | tf_op jit(solution)/shard_map/all_to_all | solution.py:251
Sparse Core Ops, SparseCore 0:
  10.1 78.4 all-gather.2
  118.1 76.5 reduce-scatter.1
